TPU v7x, 512 devices: a whole 4x8x8 slice. The times are simulated.
512 devices in a mesh: grp: 32 (over z, x_lo, core), rep: 16 (over y, x_hi).
Axes of the slice: x: 4 (x_hi: 2, x_lo: 2; x = x_hi * 2 + x_lo), y: 8, z: 8, core: 2. Of those that a mesh axis runs over, the one named last changes fastest.
Arguments:
- embeddings: bfloat16 [16, 8192, 512], P('rep', 'grp'), may hold values from -64 to 64
- cluster_of: int32 [16, 8192], P('rep', 'grp'), may hold values from 0 to 7, as said below
- cluster_rows: int32 [16, 2, 8], P('rep'), may hold values from 0 to 8192, as said below
Outputs:
- max_similarity: float32 [16, 8192], P('rep', 'grp')
Inputs may be any that keep to these rules, and one draw needn't show every extreme that they name: Along a set's rows cluster_of never falls; cluster c occupies exactly the rows cluster_rows[s, 0, c] to cluster_rows[s, 1, c] - 1, and holds at least 2 rows. `cluster_rows`: the clusters of a set tile its rows in order: cluster 0 starts at row 0, each cluster starts where the previous one ends, the last ends at 8192.
All inputs are finite; a program needn't handle non-finite values.
Results may differ from a plain program's by a relative error of at most 0.00043.
Values may be sent and summed in bfloat16 or wider, within the bound.
No kernel may reach another device: no remote copies, remote signals or barrier semaphores. Data moves between devices by JAX's collectives and lax.ppermute only.
A program may use at most 64 MiB of HBM per device.

v0:
```python
import functools

import jax
import jax.numpy as jnp
from jax import lax
from jax.experimental import pallas as pl
from jax.experimental.pallas import tpu as pltpu
from jax.sharding import Mesh, PartitionSpec as P

Z, XL, C, Y, XH = 8, 2, 2, 8, 2
GRP = ("z", "xl", "c")
REP = ("y", "xh")
ROWS = 256
CHIP = C * ROWS
PLANE = XL * CHIP
D = 512
TOTAL = Z * PLANE * Y * XH
NONE = -2.0
STEP = 256


def shift(hops):
    return [(z * C + c, (z + hops[c]) % Z * C + c) for z in range(Z) for c in range(C)]


def spread_sum(partial, axes, count):
    return lax.all_to_all(jnp.broadcast_to(partial[None], (count, 4, 128)), axes, 0, 0)


def score_kernel(
    bounds, partials, own, chip, side, two, odd, four, out, rows, cols, unit, sems
):
    z, xl, core = lax.axis_index("z"), lax.axis_index("xl"), lax.axis_index("c")
    sign = 2 * core - 1
    here = pl.multiple_of(xl * CHIP, CHIP)
    there = pl.multiple_of((1 - xl) * CHIP, CHIP)
    copies = [
        pltpu.make_async_copy(chip, rows.at[pl.ds(here, CHIP)], sems.at[0]),
        pltpu.make_async_copy(side, rows.at[pl.ds(there, CHIP)], sems.at[1]),
        pltpu.make_async_copy(own, cols.at[pl.ds(0, ROWS)], sems.at[2]),
        pltpu.make_async_copy(two, cols.at[pl.ds(ROWS, CHIP)], sems.at[3]),
        pltpu.make_async_copy(odd, cols.at[pl.ds(ROWS + CHIP, 2 * CHIP)], sems.at[4]),
        pltpu.make_async_copy(four, cols.at[pl.ds(ROWS + 3 * CHIP, ROWS)], sems.at[5]),
    ]
    for copy in copies:
        copy.start()
    total = jnp.sum(partials[...], axis=0)
    centroid = jnp.concatenate([total[k : k + 1] for k in range(4)], axis=1) / TOTAL

    def normalized(block):
        centered = block.astype(jnp.float32) - centroid
        norm = jnp.sum(centered * centered, axis=1, keepdims=True)
        return (centered * lax.rsqrt(norm + 1e-06)).astype(jnp.bfloat16)

    def cluster(position):
        member = jnp.zeros(position.shape, jnp.int32)
        for k in range(7):
            member += (position >= bounds[0, 1, k]).astype(jnp.int32)
        return member

    copies[0].wait()
    copies[1].wait()
    for k in range(PLANE // STEP):
        unit[pl.ds(k * STEP, STEP)] = normalized(rows[pl.ds(k * STEP, STEP)])
    row_position = z * PLANE + lax.broadcasted_iota(jnp.int32, (1, PLANE), 1)
    row_cluster = cluster(row_position)

    def plane_start(offset):
        return lax.rem(z + offset + Z, Z) * PLANE + xl * CHIP

    starts = [plane_start(0) + core * ROWS]
    for offset in (2 * sign, sign, 3 * sign):
        starts += [plane_start(offset), plane_start(offset) + ROWS]
    starts += [plane_start(4) + core * ROWS]
    waits = {0: 2, 1: 3, 3: 4, 7: 5}
    best = jnp.full((8, PLANE), NONE, jnp.float32)
    for k, start in enumerate(starts):
        if k in waits:
            copies[waits[k]].wait()
        piece = normalized(cols[pl.ds(k * STEP, STEP)])
        scores = lax.dot_general(
            piece, unit[...], (((1,), (1,)), ((), ())), preferred_element_type=jnp.float32
        )
        position = start + lax.broadcasted_iota(jnp.int32, (STEP, 1), 0)
        inside = cluster(position) == row_cluster
        if k == 0:
            inside &= position != row_position
        scores = jnp.where(inside, scores, NONE)
        best = jnp.maximum(best, jnp.max(scores.reshape(STEP // 8, 8, PLANE), axis=0))
    best = jnp.max(best, axis=0, keepdims=True)
    for k in range(PLANE // 128):
        out[k // 2, pl.ds(k % 2, 1)] = best[:, k * 128 : (k + 1) * 128]


def score(bounds, partials, *blocks):
    return pl.pallas_call(
        score_kernel,
        out_shape=jax.ShapeDtypeStruct((XL * C, ROWS // 128, 128), jnp.float32),
        in_specs=[
            pl.BlockSpec(memory_space=pltpu.SMEM),
            pl.BlockSpec(memory_space=pltpu.VMEM),
        ]
        + [pl.BlockSpec(memory_space=pl.ANY)] * len(blocks),
        out_specs=pl.BlockSpec(memory_space=pltpu.VMEM),
        scratch_shapes=[
            pltpu.VMEM((PLANE, D), jnp.bfloat16),
            pltpu.VMEM((2 * PLANE, D), jnp.bfloat16),
            pltpu.VMEM((PLANE, D), jnp.bfloat16),
            pltpu.SemaphoreType.DMA((6,)),
        ],
        compiler_params=pltpu.CompilerParams(vmem_limit_bytes=32 * 1024 * 1024),
        cost_estimate=pl.CostEstimate(
            flops=2 * PLANE * 2 * PLANE * D, bytes_accessed=3 * PLANE * D * 2, transcendentals=0
        ),
        name="score",
    )(bounds, partials, *blocks)


def on_device(embeddings, cluster_rows):
    own = embeddings[0]
    chip = lax.all_gather(own, "c", axis=0, tiled=True)
    two = lax.ppermute(chip, ("z", "c"), shift((2, -2)))
    side = lax.ppermute(chip, "xl", [(0, 1), (1, 0)])
    column_sums = jnp.sum(chip, axis=0, dtype=jnp.float32).reshape(4, 128)
    set_sums = jnp.sum(spread_sum(column_sums, ("z", "xl"), Z * XL), axis=0)
    two, set_sums = lax.optimization_barrier((two, set_sums))
    odd = lax.ppermute(jnp.concatenate([chip, two], axis=0), ("z", "c"), shift((1, -1)))
    half = lax.dynamic_slice_in_dim(two, lax.axis_index("c") * ROWS, ROWS, 0)
    four = lax.ppermute(half, ("z", "c"), shift((2, -2)))
    partials = spread_sum(set_sums, REP, Y * XH)
    best = score(cluster_rows, partials, own, chip, side, two, odd, four)
    best = lax.all_to_all(best, ("xl", "c"), 0, 0)
    return jnp.max(best, axis=0).reshape(1, ROWS)


def solution(mesh):
    fine = Mesh(mesh.devices.reshape(Z, XL, C, Y, XH), (*GRP, *REP))
    inner = jax.shard_map(
        on_device,
        mesh=fine,
        in_specs=(P(REP, GRP, None), P(REP, None, None)),
        out_specs=P(REP, GRP),
        check_vma=False,
    )

    def run(embeddings, cluster_of, cluster_rows):
        del cluster_of
        return inner(embeddings, cluster_rows)

    return run
```

profile of v0, /device:TPU:1, one launch (start us, length us, event | category | flops | bytes accessed | tf_op | source)
XLA Modules:
  0.0 71.2 jit_solution(12461479730753511285)
XLA Ops:
  0.0 8.9 %all-gather = bf16[1,512,512]{2,1,0:T(8,128)(2,1)S(1)} all-gather(bf16[1,256,512]{2,1,0:T(8,128)(2,1)} %param.3), channel_id=2, replica_groups=mesh['z'=8,'xl'=2,'c'=2,'y'=8,'xh'=2] {'c'}, dimensions={1}, use_global_device_ids=true | all-gather | bytes 786432 | tf_op jit(solution)/shard_map/all_gather | solution.py:121
  8.9 5.3 %collective-permute-start = (bf16[512,512]{1,0:T(8,128)(2,1)S(1)}, bf16[512,512]{1,0:T(8,128)(2,1)S(1)}, u32[]{:S(2)}, u32[]{:S(2)}) collective-permute-start(bf16[512,512]{1,0:T(8,128)(2,1)S(1)} %bitcast.5), channel_id=1, source_target_pairs={{0,128},{16,400},{64,192},{80,464},{128,256},{144,16},{192,320},{2... | collective-permute-start | bytes 1572872 | tf_op jit(solution)/shard_map/ppermute | solution.py:122
  14.2 0.1 convert_reduce_fusion
  14.3 14.8 %all_to_all.15 = f32[16,4,128]{2,1,0:T(4,128)S(1)} all-to-all(f32[16,4,128]{2,1,0:T(4,128)S(1)} %broadcast_in_dim.14), channel_id=1, replica_groups=mesh['z'=8,'xl'=2,'c'=2,'y'=8,'xh'=2] {'z','xl'}, dimensions={0} | all-to-all | bytes 65536 | tf_op jit(solution)/shard_map/all_to_all | solution.py:27
  29.1 0.0 copy-start
  29.2 0.0 copy-start.1
  29.2 0.0 collective-permute-done.two
  29.2 1.1 %pad_maximum_fusion = bf16[1024,512]{1,0:T(8,128)(2,1)} fusion(bf16[512,512]{1,0:T(8,128)(2,1)S(1)} %collective-permute-done.two, bf16[512,512]{1,0:T(8,128)(2,1)S(1)} %bitcast.6), kind=kLoop, calls=%fused_computation | loop fusion | flops 2097152 | bytes 2097152 | tf_op jit(solution)/shard_map/concatenate | solution.py:127
  30.2 3.4 %collective-permute-start.2 = (bf16[1024,512]{1,0:T(8,128)(2,1)}, bf16[1024,512]{1,0:T(8,128)(2,1)S(1)}, u32[]{:S(2)}, u32[]{:S(2)}) collective-permute-start(bf16[1024,512]{1,0:T(8,128)(2,1)} %pad_maximum_fusion), channel_id=1, source_target_pairs={{0,64},{16,464},{64,128},{80,16},{128,192},{144,80},{192,256},{208... | collective-permute-start | bytes 3145736 | tf_op jit(solution)/shard_map/ppermute | solution.py:127
  33.6 2.5 %collective-permute-start.1 = (bf16[512,512]{1,0:T(8,128)(2,1)S(1)}, bf16[512,512]{1,0:T(8,128)(2,1)S(1)}, u32[]{:S(2)}, u32[]{:S(2)}) collective-permute-start(bf16[512,512]{1,0:T(8,128)(2,1)S(1)} %bitcast.7), channel_id=1, source_target_pairs={{0,32},{32,0},{1,33},{33,1},{2,34},{34,2},{3,35},{35,3},{4,36},{36... | collective-permute-start | bytes 1572872 | tf_op jit(solution)/shard_map/ppermute | solution.py:123
  36.2 3.9 %collective-permute-start.3 = (bf16[256,512]{1,0:T(8,128)(2,1)S(1)}, bf16[256,512]{1,0:T(8,128)(2,1)S(1)}, u32[]{:S(2)}, u32[]{:S(2)}) collective-permute-start(bf16[256,512]{1,0:T(8,128)(2,1)S(1)} %constant_dynamic-slice_fusion), channel_id=1, source_target_pairs={{0,128},{16,400},{64,192},{80,464},{128,256},{144,16},{192,320},{2... | collective-permute-start | bytes 786440 | tf_op jit(solution)/shard_map/ppermute | solution.py:129
  40.0 0.6 broadcast_in_dim.15
  40.6 9.3 %all-to-all-start.1 = ((f32[16,4,128]{2,1,0:T(4,128)}), f32[16,4,128]{2,1,0:T(4,128)S(1)}, u32[]{:S(2)}, u32[]{:S(2)}) async-start(f32[16,4,128]{2,1,0:T(4,128)} %broadcast_in_dim.15), calls=%async_computation.1 | async-start | bytes 65536 | tf_op jit(solution)/shard_map/all_to_all | solution.py:27
  50.0 0.0 collective-permute-done.1.side
  50.0 9.1 %all-to-all-done.1.partials = f32[16,4,128]{2,1,0:T(4,128)S(1)} async-done(((f32[16,4,128]{2,1,0:T(4,128)}), f32[16,4,128]{2,1,0:T(4,128)S(1)}, u32[]{:S(2)}, u32[]{:S(2)}) %all-to-all-start.1) | async-done | bytes 32800 | tf_op jit(solution)/shard_map/all_to_all | solution.py:27
  59.1 0.0 collective-permute-done.3.four
  59.1 0.0 collective-permute-done.2.odd
  59.1 0.0 copy-done
  59.1 0.0 copy-done.1
  59.1 5.0 %score.1 = f32[4,2,128]{2,1,0:T(2,128)S(1)} custom-call(s32[1,2,8]{2,1,0:T(2,128)S(1)} %copy-done.1, f32[16,4,128]{2,1,0:T(4,128)S(1)} %all-to-all-done.1.partials, bf16[256,512]{1,0:T(8,128)(2,1)S(1)} %bitcast.9, bf16[512,512]{1,0:T(8,128)(2,1)S(1)} %bitcast.8, bf16[512,512]{1,0:T(8,128)(2,1)S(1)} %collective-permute-done.1.side, ...), custom_call_target="tpu_custom_call" | custom-call | flops 2147483648 | bytes 3145728 | tf_op jit(solution)/shard_map/score/pallas_call | solution.py:96
  64.2 6.5 %all_to_all.16 = f32[4,2,128]{2,1,0:T(2,128)S(1)} all-to-all(f32[4,2,128]{2,1,0:T(2,128)S(1)} %score.1), channel_id=1, replica_groups=mesh['z'=8,'xl'=2,'c'=2,'y'=8,'xh'=2] {'xl','c'}, dimensions={0} | all-to-all | bytes 8192 | tf_op jit(solution)/shard_map/all_to_all | solution.py:132
  70.6 0.6 reduce_max.9
  (3 shorter events, 0.1 us)
Async XLA Ops:
  8.9 20.3 %collective-permute-start = (bf16[512,512]{1,0:T(8,128)(2,1)S(1)}, bf16[512,512]{1,0:T(8,128)(2,1)S(1)}, u32[]{:S(2)}, u32[]{:S(2)}) collective-permute-start(bf16[512,512]{1,0:T(8,128)(2,1)S(1)} %bitcast.5), channel_id=1, source_target_pairs={{0,128},{16,400},{64,192},{80,464},{128,256},{144,16},{192,320},{2... | collective-permute-start | bytes 1572872 | tf_op jit(solution)/shard_map/ppermute | solution.py:122
  29.1 29.9 %copy-start = (bf16[1,256,512]{2,1,0:T(8,128)(2,1)S(1)}, bf16[1,256,512]{2,1,0:T(8,128)(2,1)}, u32[]{:S(2)}) copy-start(bf16[1,256,512]{2,1,0:T(8,128)(2,1)} %param.3) | copy-start | bytes 786436
  29.2 29.9 %copy-start.1 = (s32[1,2,8]{2,1,0:T(2,128)S(1)}, s32[1,2,8]{2,1,0:T(2,128)}, u32[]{:S(2)}) copy-start(s32[1,2,8]{2,1,0:T(2,128)} %bounds.1) | copy-start | bytes 196
  30.2 28.9 %collective-permute-start.2 = (bf16[1024,512]{1,0:T(8,128)(2,1)}, bf16[1024,512]{1,0:T(8,128)(2,1)S(1)}, u32[]{:S(2)}, u32[]{:S(2)}) collective-permute-start(bf16[1024,512]{1,0:T(8,128)(2,1)} %pad_maximum_fusion), channel_id=1, source_target_pairs={{0,64},{16,464},{64,128},{80,16},{128,192},{144,80},{192,256},{208... | collective-permute-start | bytes 3145736 | tf_op jit(solution)/shard_map/ppermute | solution.py:127
  33.6 16.3 %collective-permute-start.1 = (bf16[512,512]{1,0:T(8,128)(2,1)S(1)}, bf16[512,512]{1,0:T(8,128)(2,1)S(1)}, u32[]{:S(2)}, u32[]{:S(2)}) collective-permute-start(bf16[512,512]{1,0:T(8,128)(2,1)S(1)} %bitcast.7), channel_id=1, source_target_pairs={{0,32},{32,0},{1,33},{33,1},{2,34},{34,2},{3,35},{35,3},{4,36},{36... | collective-permute-start | bytes 1572872 | tf_op jit(solution)/shard_map/ppermute | solution.py:123
  36.2 22.9 %collective-permute-start.3 = (bf16[256,512]{1,0:T(8,128)(2,1)S(1)}, bf16[256,512]{1,0:T(8,128)(2,1)S(1)}, u32[]{:S(2)}, u32[]{:S(2)}) collective-permute-start(bf16[256,512]{1,0:T(8,128)(2,1)S(1)} %constant_dynamic-slice_fusion), channel_id=1, source_target_pairs={{0,128},{16,400},{64,192},{80,464},{128,256},{144,16},{192,320},{2... | collective-permute-start | bytes 786440 | tf_op jit(solution)/shard_map/ppermute | solution.py:129
  40.6 18.5 %all-to-all-start.1 = ((f32[16,4,128]{2,1,0:T(4,128)}), f32[16,4,128]{2,1,0:T(4,128)S(1)}, u32[]{:S(2)}, u32[]{:S(2)}) async-start(f32[16,4,128]{2,1,0:T(4,128)} %broadcast_in_dim.15), calls=%async_computation.1 | async-start | bytes 65536 | tf_op jit(solution)/shard_map/all_to_all | solution.py:27
where the time goes:
time: 71.5 us; the launch traced here: 71.2 us
  blocking collectives  30.2 us (42%)
  starting transfers between devices  24.3 us (34%)
  waiting for transfers between devices  9.13 us (13%)
  Pallas kernels  5.04 us (7%)
  other arithmetic  1.78 us (2%)
    all_to_all x1, blocking collectives, spread_sum(): lax.all_to_all(jnp.broadcast_to(partial[None], (count, 4, 128)), axes, 0, 0)  14.8 us
    all_to_all x1, starting transfers between devices, spread_sum(): lax.all_to_all(jnp.broadcast_to(partial[None], (count, 4, 128)), axes, 0, 0)  9.32 us
    all_to_all x1, waiting for transfers between devices, spread_sum(): lax.all_to_all(jnp.broadcast_to(partial[None], (count, 4, 128)), axes, 0, 0)  9.12 us
    all_gather x1, blocking collectives, on_device(): chip = lax.all_gather(own, 'c', axis=0, tiled=True)  8.89 us
    all_to_all x1, blocking collectives, on_device(): best = lax.all_to_all(best, ('xl', 'c'), 0, 0)  6.45 us
    ppermute x1, starting transfers between devices, on_device(): two = lax.ppermute(chip, ('z', 'c'), shift((2, -2)))  5.27 us
    pallas_call x1, Pallas kernels, score(): pl.pallas_call(score_kernel, out_shape=jax.ShapeDtypeStruct((XL * C, ROWS...  5.04 us
    ppermute x1, starting transfers between devices, on_device(): four = lax.ppermute(half, ('z', 'c'), shift((2, -2)))  3.86 us
  transfers between devices with their start and end apart: 5, of which 1 were waited for; matrix products, arithmetic and copies ran while one was open for 1% of the time, Pallas kernels for 0%

commit v1 on v0

v1 whole, which is shorter than its diff:
```python
import jax
import jax.numpy as jnp
from jax import lax
from jax.experimental import pallas as pl
from jax.experimental.pallas import tpu as pltpu
from jax.sharding import Mesh, PartitionSpec as P

Z, XL, C, Y, XH = 8, 2, 2, 8, 2
GRP = ("z", "xl", "c")
REP = ("y", "xh")
ROWS = 256
CHIP = C * ROWS
PLANE = XL * CHIP
D = 512
TOTAL = Z * PLANE * Y * XH
NONE = -2.0
STEP = 256


def shift(hops):
    return [(z * C + c, (z + hops[c]) % Z * C + c) for z in range(Z) for c in range(C)]


def spread_sum(partial, axes, count):
    return lax.all_to_all(jnp.broadcast_to(partial[None], (count, 4, 128)), axes, 0, 0)


def plane_start(z, xl, offset):
    return lax.rem(z + offset + Z, Z) * PLANE + xl * CHIP


def normalizer(partials):
    total = jnp.sum(partials[...], axis=0)
    centroid = jnp.concatenate([total[k : k + 1] for k in range(4)], axis=1) / TOTAL

    def normalized(block):
        centered = block.astype(jnp.float32) - centroid
        norm = jnp.sum(centered * centered, axis=1, keepdims=True)
        return (centered * lax.rsqrt(norm + 1e-06)).astype(jnp.bfloat16)

    return normalized


def cluster_by(bounds, position):
    member = jnp.zeros(position.shape, jnp.int32)
    for k in range(7):
        member += (position >= bounds[0, 1, k]).astype(jnp.int32)
    return member


def raise_best(best, bounds, unit, piece, start, z, diagonal=False):
    row_position = z * PLANE + lax.broadcasted_iota(jnp.int32, (1, PLANE), 1)
    scores = lax.dot_general(
        piece, unit[...], (((1,), (1,)), ((), ())), preferred_element_type=jnp.float32
    )
    position = start + lax.broadcasted_iota(jnp.int32, (STEP, 1), 0)
    inside = cluster_by(bounds, position) == cluster_by(bounds, row_position)
    if diagonal:
        inside &= position != row_position
    scores = jnp.where(inside, scores, NONE)
    return jnp.maximum(best, jnp.max(scores.reshape(STEP // 8, 8, PLANE), axis=0))


def near_kernel(
    bounds, partials, own, chip, side, two, one, unit, best, rows, cols, sems
):
    z, xl, core = lax.axis_index("z"), lax.axis_index("xl"), lax.axis_index("c")
    sign = 2 * core - 1
    here = pl.multiple_of(xl * CHIP, CHIP)
    there = pl.multiple_of((1 - xl) * CHIP, CHIP)
    copies = [
        pltpu.make_async_copy(chip, rows.at[pl.ds(here, CHIP)], sems.at[0]),
        pltpu.make_async_copy(side, rows.at[pl.ds(there, CHIP)], sems.at[1]),
        pltpu.make_async_copy(own, cols.at[pl.ds(0, ROWS)], sems.at[2]),
        pltpu.make_async_copy(two, cols.at[pl.ds(ROWS, CHIP)], sems.at[3]),
        pltpu.make_async_copy(one, cols.at[pl.ds(ROWS + CHIP, CHIP)], sems.at[4]),
    ]
    for copy in copies:
        copy.start()
    normalized = normalizer(partials)
    copies[0].wait()
    copies[1].wait()
    for k in range(PLANE // STEP):
        unit[pl.ds(k * STEP, STEP)] = normalized(rows[pl.ds(k * STEP, STEP)])
    starts = [plane_start(z, xl, 0) + core * ROWS]
    for offset in (2 * sign, sign):
        starts += [plane_start(z, xl, offset), plane_start(z, xl, offset) + ROWS]
    waits = {0: 2, 1: 3, 3: 4}
    found = jnp.full((8, PLANE), NONE, jnp.float32)
    for k, start in enumerate(starts):
        if k in waits:
            copies[waits[k]].wait()
        piece = normalized(cols[pl.ds(k * STEP, STEP)])
        found = raise_best(found, bounds, unit, piece, start, z, k == 0)
    best[...] = found


def far_kernel(bounds, partials, unit, best, three, four, out, cols, sems):
    z, xl, core = lax.axis_index("z"), lax.axis_index("xl"), lax.axis_index("c")
    sign = 2 * core - 1
    copies = [
        pltpu.make_async_copy(three, cols.at[pl.ds(0, CHIP)], sems.at[0]),
        pltpu.make_async_copy(four, cols.at[pl.ds(CHIP, ROWS)], sems.at[1]),
    ]
    for copy in copies:
        copy.start()
    normalized = normalizer(partials)
    starts = [plane_start(z, xl, 3 * sign), plane_start(z, xl, 3 * sign) + ROWS]
    starts += [plane_start(z, xl, 4) + core * ROWS]
    found = best[...]
    for k, start in enumerate(starts):
        if k == 0:
            copies[0].wait()
        if k == 2:
            copies[1].wait()
        piece = normalized(cols[pl.ds(k * STEP, STEP)])
        found = raise_best(found, bounds, unit, piece, start, z)
    found = jnp.max(found, axis=0, keepdims=True)
    for k in range(PLANE // 128):
        out[k // 2, pl.ds(k % 2, 1)] = found[:, k * 128 : (k + 1) * 128]


IN_VMEM = pl.BlockSpec(memory_space=pltpu.VMEM)
ANYWHERE = pl.BlockSpec(memory_space=pl.ANY)
PARAMS = pltpu.CompilerParams(vmem_limit_bytes=32 * 1024 * 1024)


def cost(flops):
    return pl.CostEstimate(flops=int(flops), bytes_accessed=4 * 2**20, transcendentals=0)


def near(bounds, partials, *blocks):
    return pl.pallas_call(
        near_kernel,
        out_shape=(
            jax.ShapeDtypeStruct((PLANE, D), jnp.bfloat16),
            jax.ShapeDtypeStruct((8, PLANE), jnp.float32),
        ),
        in_specs=[pl.BlockSpec(memory_space=pltpu.SMEM), IN_VMEM] + [ANYWHERE] * 5,
        out_specs=(IN_VMEM, IN_VMEM),
        scratch_shapes=[
            pltpu.VMEM((PLANE, D), jnp.bfloat16),
            pltpu.VMEM((ROWS + 2 * CHIP, D), jnp.bfloat16),
            pltpu.SemaphoreType.DMA((5,)),
        ],
        compiler_params=PARAMS,
        cost_estimate=cost(5e9),
        name="near",
    )(bounds, partials, *blocks)


def far(bounds, partials, unit, best, three, four):
    return pl.pallas_call(
        far_kernel,
        out_shape=jax.ShapeDtypeStruct((XL * C, ROWS // 128, 128), jnp.float32),
        in_specs=[pl.BlockSpec(memory_space=pltpu.SMEM)] + [IN_VMEM] * 3 + [ANYWHERE] * 2,
        out_specs=IN_VMEM,
        scratch_shapes=[
            pltpu.VMEM((CHIP + ROWS, D), jnp.bfloat16),
            pltpu.SemaphoreType.DMA((2,)),
        ],
        compiler_params=PARAMS,
        cost_estimate=cost(1e9),
        name="far",
    )(bounds, partials, unit, best, three, four)


def resend(received, count, flops):
    def kernel(received, out):
        total = jnp.sum(received[...], axis=0, keepdims=True)
        out[...] = jnp.broadcast_to(total, out.shape)

    return pl.pallas_call(
        kernel,
        out_shape=jax.ShapeDtypeStruct((count, 4, 128), jnp.float32),
        in_specs=[IN_VMEM],
        out_specs=IN_VMEM,
        cost_estimate=cost(flops),
        name="resend",
    )(received)


def on_device(embeddings, cluster_rows):
    own = embeddings[0]
    chip = lax.all_gather(own, "c", axis=0, tiled=True)
    two = lax.ppermute(chip, ("z", "c"), shift((2, -2)))
    one = lax.ppermute(chip, ("z", "c"), shift((1, -1)))
    side = lax.ppermute(chip, "xl", [(0, 1), (1, 0)])
    column_sums = jnp.sum(chip, axis=0, dtype=jnp.float32).reshape(4, 128)
    sums = spread_sum(column_sums, ("z", "xl", "xh"), Z * XL * XH)
    three = lax.ppermute(two, ("z", "c"), shift((1, -1)))
    sums = resend(sums, Y, 8000000000)
    half = lax.dynamic_slice_in_dim(three, lax.axis_index("c") * ROWS, ROWS, 0)
    four = lax.ppermute(half, ("z", "c"), shift((1, -1)))
    partials = lax.all_to_all(sums, "y", 0, 0)
    unit, best = near(cluster_rows, partials, own, chip, side, two, one)
    best = far(cluster_rows, partials, unit, best, three, four)
    best = lax.all_to_all(best, ("xl", "c"), 0, 0)
    return jnp.max(best, axis=0).reshape(1, ROWS)


def solution(mesh):
    fine = Mesh(mesh.devices.reshape(Z, XL, C, Y, XH), (*GRP, *REP))
    inner = jax.shard_map(
        on_device,
        mesh=fine,
        in_specs=(P(REP, GRP, None), P(REP, None, None)),
        out_specs=P(REP, GRP),
        check_vma=False,
    )

    def run(embeddings, cluster_of, cluster_rows):
        del cluster_of
        return inner(embeddings, cluster_rows)

    return run
```

time: 71.5 us -> 62.6 us (0.88)
  blocking collectives: 30.2 us -> 18.3 us
  starting transfers between devices: 24.3 us -> 32.7 us
  waiting for transfers between devices: 9.13 us -> 1.87 us
  Pallas kernels: 5.04 us -> 7.22 us
  other arithmetic: 1.78 us -> 0.69 us
    all_to_all x1 -> x0, blocking collectives: 14.8 us -> none  [spread_sum(): lax.all_to_all(jnp.broadcast_to(partial[None], (count, 4, 128)), axes, 0, 0)]
    all_to_all x1, waiting for transfers between devices: 9.12 us -> 0.01 us  [spread_sum(): lax.all_to_all(jnp.broadcast_to(partial[None], (count, 4, 128)), axes, 0, 0)]
    ppermute x2 -> x3, starting transfers between devices: 7.27 us -> 13.4 us  [the longest x1 4.7 us: on_device(): four = lax.ppermute(half, ('z', 'c'), shift((1, -1)))]
    all_to_all x0 -> x1, starting transfers between devices: none -> 5.56 us  [on_device(): partials = lax.all_to_all(sums, 'y', 0, 0)]
    all_to_all x1, starting transfers between devices: 9.32 us -> 5.32 us  [spread_sum(): lax.all_to_all(jnp.broadcast_to(partial[None], (count, 4, 128)), axes, 0, 0)]
    all_to_all x1, blocking collectives: 6.45 us -> 9.37 us  [on_device(): best = lax.all_to_all(best, ('xl', 'c'), 0, 0)]
    pallas_call x1 -> x3, Pallas kernels: 5.04 us -> 7.22 us  [the longest x1 3.65 us: near(): pl.pallas_call(near_kernel, out_shape=(jax.ShapeDtypeStruct((PLANE, D), j...]
    all_to_all x0 -> x1, waiting for transfers between devices: none -> 1.85 us  [on_device(): partials = lax.all_to_all(sums, 'y', 0, 0)]
  transfers between devices with their start and end apart: 5 -> 7, of which waited for: 1 -> 1; matrix products, arithmetic and copies ran while one was open for 1% -> 1% of each run, Pallas kernels for 0% -> 8%
where the time goes in v1:
time: 62.6 us; the launch traced here: 62.2 us
  starting transfers between devices  32.7 us (52%)
  blocking collectives  18.3 us (29%)
  Pallas kernels  7.22 us (12%)
  waiting for transfers between devices  1.87 us (3%)
  local copies, waits for them, and re-layouts  1.28 us (2%)
  other arithmetic  0.69 us (1%)
    all_to_all x1, blocking collectives, on_device(): best = lax.all_to_all(best, ('xl', 'c'), 0, 0)  9.37 us
    all_gather x1, blocking collectives, on_device(): chip = lax.all_gather(own, 'c', axis=0, tiled=True)  8.89 us
    all_to_all x1, starting transfers between devices, on_device(): partials = lax.all_to_all(sums, 'y', 0, 0)  5.56 us
    all_to_all x1, starting transfers between devices, spread_sum(): lax.all_to_all(jnp.broadcast_to(partial[None], (count, 4, 128)), axes, 0, 0)  5.32 us
    ppermute x1, starting transfers between devices, on_device(): two = lax.ppermute(chip, ('z', 'c'), shift((2, -2)))  5.27 us
    ppermute x1, starting transfers between devices, on_device(): four = lax.ppermute(half, ('z', 'c'), shift((1, -1)))  4.7 us
    ppermute x1, starting transfers between devices, on_device(): one = lax.ppermute(chip, ('z', 'c'), shift((1, -1)))  4.39 us
    ppermute x1, starting transfers between devices, on_device(): three = lax.ppermute(two, ('z', 'c'), shift((1, -1)))  4.32 us
  transfers between devices with their start and end apart: 7, of which 1 were waited for; matrix products, arithmetic and copies ran while one was open for 1% of the time, Pallas kernels for 8%

profile of v1, /device:TPU:1, one launch (start us, length us, event | category | flops | bytes accessed | tf_op | source)
XLA Modules:
  0.0 62.2 jit_solution(4471780709099893815)
XLA Ops:
  0.0 8.9 %all-gather = bf16[1,512,512]{2,1,0:T(8,128)(2,1)S(1)} all-gather(bf16[1,256,512]{2,1,0:T(8,128)(2,1)} %param.3), channel_id=2, replica_groups=mesh['z'=8,'xl'=2,'c'=2,'y'=8,'xh'=2] {'c'}, dimensions={1}, use_global_device_ids=true | all-gather | bytes 786432 | tf_op jit(solution)/shard_map/all_gather | solution.py:185
  8.9 5.3 %collective-permute-start.1 = (bf16[512,512]{1,0:T(8,128)(2,1)S(1)}, bf16[512,512]{1,0:T(8,128)(2,1)S(1)}, u32[]{:S(2)}, u32[]{:S(2)}) collective-permute-start(bf16[512,512]{1,0:T(8,128)(2,1)S(1)} %bitcast.5), channel_id=1, source_target_pairs={{0,128},{16,400},{64,192},{80,464},{128,256},{144,16},{192,320},{2... | collective-permute-start | bytes 1572872 | tf_op jit(solution)/shard_map/ppermute | solution.py:186
  14.2 0.1 convert_reduce_fusion
  14.3 0.6 %broadcast_in_dim.8 = f32[32,4,128]{2,1,0:T(4,128)} broadcast(f32[4,128]{1,0:T(4,128)S(1)} %bitcast.10), dimensions={1,2} | broadcast | bytes 67584 | tf_op jit(solution)/shard_map/broadcast_in_dim | solution.py:25
  14.9 5.3 %all-to-all-start = ((f32[32,4,128]{2,1,0:T(4,128)}), f32[32,4,128]{2,1,0:T(4,128)S(1)}, u32[]{:S(2)}, u32[]{:S(2)}) async-start(f32[32,4,128]{2,1,0:T(4,128)} %broadcast_in_dim.8), calls=%async_computation | async-start | bytes 131072 | tf_op jit(solution)/shard_map/all_to_all | solution.py:25
  20.2 3.1 %collective-permute-start = (bf16[512,512]{1,0:T(8,128)(2,1)S(1)}, bf16[512,512]{1,0:T(8,128)(2,1)S(1)}, u32[]{:S(2)}, u32[]{:S(2)}) collective-permute-start(bf16[512,512]{1,0:T(8,128)(2,1)S(1)} %bitcast.6), channel_id=1, source_target_pairs={{0,32},{32,0},{1,33},{33,1},{2,34},{34,2},{3,35},{35,3},{4,36},{36... | collective-permute-start | bytes 1572872 | tf_op jit(solution)/shard_map/ppermute | solution.py:188
  23.4 4.4 %collective-permute-start.2 = (bf16[512,512]{1,0:T(8,128)(2,1)S(1)}, bf16[512,512]{1,0:T(8,128)(2,1)S(1)}, u32[]{:S(2)}, u32[]{:S(2)}) collective-permute-start(bf16[512,512]{1,0:T(8,128)(2,1)S(1)} %bitcast.7), channel_id=1, source_target_pairs={{0,64},{16,464},{64,128},{80,16},{128,192},{144,80},{192,256},{208... | collective-permute-start | bytes 1572872 | tf_op jit(solution)/shard_map/ppermute | solution.py:187
  27.8 0.0 collective-permute-done.1.two
  27.8 4.3 %collective-permute-start.3 = (bf16[512,512]{1,0:T(8,128)(2,1)S(1)}, bf16[512,512]{1,0:T(8,128)(2,1)S(1)}, u32[]{:S(2)}, u32[]{:S(2)}) collective-permute-start(bf16[512,512]{1,0:T(8,128)(2,1)S(1)} %collective-permute-done.1.two), channel_id=1, source_target_pairs={{0,64},{16,464},{64,128},{80,16},{128,192},{144,80},{192,256},{208... | collective-permute-start | bytes 1572872 | tf_op jit(solution)/shard_map/ppermute | solution.py:191
  32.1 0.0 all-to-all-done.received
  32.1 0.0 copy-start.2
  32.1 0.6 copy-done.2
  32.8 1.5 %resend.1 = f32[8,4,128]{2,1,0:T(4,128)} custom-call(f32[32,4,128]{2,1,0:T(4,128)} %copy-done.2), custom_call_target="tpu_custom_call" | custom-call | flops 8000000000 | bytes 4194304 | tf_op jit(solution)/shard_map/resend/pallas_call | solution.py:173
  34.2 5.6 %all-to-all-start.1 = ((f32[8,4,128]{2,1,0:T(4,128)}), f32[8,4,128]{2,1,0:T(4,128)S(1)}, u32[]{:S(2)}, u32[]{:S(2)}) async-start(f32[8,4,128]{2,1,0:T(4,128)} %resend.1), calls=%async_computation.1 | async-start | bytes 32768 | tf_op jit(solution)/shard_map/all_to_all | solution.py:195
  39.8 0.0 copy-start
  39.8 0.0 collective-permute-done.3.three
  39.8 0.0 copy-start.1
  39.9 4.7 %collective-permute-start.4 = (bf16[256,512]{1,0:T(8,128)(2,1)S(1)}, bf16[256,512]{1,0:T(8,128)(2,1)S(1)}, u32[]{:S(2)}, u32[]{:S(2)}) collective-permute-start(bf16[256,512]{1,0:T(8,128)(2,1)S(1)} %constant_dynamic-slice_fusion), channel_id=1, source_target_pairs={{0,64},{16,464},{64,128},{80,16},{128,192},{144,80},{192,256},{208... | collective-permute-start | bytes 786440 | tf_op jit(solution)/shard_map/ppermute | solution.py:194
  44.6 1.9 %all-to-all-done.1.partials = f32[8,4,128]{2,1,0:T(4,128)S(1)} async-done(((f32[8,4,128]{2,1,0:T(4,128)}), f32[8,4,128]{2,1,0:T(4,128)S(1)}, u32[]{:S(2)}, u32[]{:S(2)}) %all-to-all-start.1) | async-done | bytes 16416 | tf_op jit(solution)/shard_map/all_to_all | solution.py:195
  46.4 0.0 collective-permute-done.side
  46.4 0.0 collective-permute-done.2.one
  46.4 0.0 copy-done
  46.4 0.0 copy-done.1
  46.4 3.6 %near.1 = (bf16[1024,512]{1,0:T(8,128)(2,1)S(1)}, f32[8,1024]{1,0:T(8,128)S(1)}) custom-call(s32[1,2,8]{2,1,0:T(2,128)S(1)} %copy-done.1, f32[8,4,128]{2,1,0:T(4,128)S(1)} %all-to-all-done.1.partials, bf16[256,512]{1,0:T(8,128)(2,1)S(1)} %bitcast.9, bf16[512,512]{1,0:T(8,128)(2,1)S(1)} %bitcast.8, bf16[512,512]{1,0:T(8,128)(2,1)S(1)} %collective-permute-done.side, ...), custom_call_target="tpu_custom_call" | custom-call | flops 5000000000 | bytes 4194304 | tf_op jit(solution)/shard_map/near/pallas_call | solution.py:133
  50.1 0.0 collective-permute-done.4.four
  50.1 2.1 %far.1 = f32[4,2,128]{2,1,0:T(2,128)S(1)} custom-call(s32[1,2,8]{2,1,0:T(2,128)S(1)} %copy-done.1, f32[8,4,128]{2,1,0:T(4,128)S(1)} %all-to-all-done.1.partials, bf16[1024,512]{1,0:T(8,128)(2,1)S(1)} %get-tuple-element.7.unit, f32[8,1024]{1,0:T(8,128)S(1)} %get-tuple-element.8.best, bf16[512,512]{1,0:T(8,128)(2,1)S(1)} %collective-permute-done.3.three, ...), custom_call_target="tpu_custom_call" | custom-call | flops 1000000000 | bytes 4194304 | tf_op jit(solution)/shard_map/far/pallas_call | solution.py:153
  52.2 9.4 %all_to_all.15 = f32[4,2,128]{2,1,0:T(2,128)S(1)} all-to-all(f32[4,2,128]{2,1,0:T(2,128)S(1)} %far.1), channel_id=1, replica_groups=mesh['z'=8,'xl'=2,'c'=2,'y'=8,'xh'=2] {'xl','c'}, dimensions={0} | all-to-all | bytes 8192 | tf_op jit(solution)/shard_map/all_to_all | solution.py:198
  61.6 0.6 reduce_max.9
  (1 shorter events, 0.0 us)
Async XLA Ops:
  8.9 18.9 %collective-permute-start.1 = (bf16[512,512]{1,0:T(8,128)(2,1)S(1)}, bf16[512,512]{1,0:T(8,128)(2,1)S(1)}, u32[]{:S(2)}, u32[]{:S(2)}) collective-permute-start(bf16[512,512]{1,0:T(8,128)(2,1)S(1)} %bitcast.5), channel_id=1, source_target_pairs={{0,128},{16,400},{64,192},{80,464},{128,256},{144,16},{192,320},{2... | collective-permute-start | bytes 1572872 | tf_op jit(solution)/shard_map/ppermute | solution.py:186
  14.9 17.2 %all-to-all-start = ((f32[32,4,128]{2,1,0:T(4,128)}), f32[32,4,128]{2,1,0:T(4,128)S(1)}, u32[]{:S(2)}, u32[]{:S(2)}) async-start(f32[32,4,128]{2,1,0:T(4,128)} %broadcast_in_dim.8), calls=%async_computation | async-start | bytes 131072 | tf_op jit(solution)/shard_map/all_to_all | solution.py:25
  20.2 26.2 %collective-permute-start = (bf16[512,512]{1,0:T(8,128)(2,1)S(1)}, bf16[512,512]{1,0:T(8,128)(2,1)S(1)}, u32[]{:S(2)}, u32[]{:S(2)}) collective-permute-start(bf16[512,512]{1,0:T(8,128)(2,1)S(1)} %bitcast.6), channel_id=1, source_target_pairs={{0,32},{32,0},{1,33},{33,1},{2,34},{34,2},{3,35},{35,3},{4,36},{36... | collective-permute-start | bytes 1572872 | tf_op jit(solution)/shard_map/ppermute | solution.py:188
  23.4 23.0 %collective-permute-start.2 = (bf16[512,512]{1,0:T(8,128)(2,1)S(1)}, bf16[512,512]{1,0:T(8,128)(2,1)S(1)}, u32[]{:S(2)}, u32[]{:S(2)}) collective-permute-start(bf16[512,512]{1,0:T(8,128)(2,1)S(1)} %bitcast.7), channel_id=1, source_target_pairs={{0,64},{16,464},{64,128},{80,16},{128,192},{144,80},{192,256},{208... | collective-permute-start | bytes 1572872 | tf_op jit(solution)/shard_map/ppermute | solution.py:187
  27.8 12.0 %collective-permute-start.3 = (bf16[512,512]{1,0:T(8,128)(2,1)S(1)}, bf16[512,512]{1,0:T(8,128)(2,1)S(1)}, u32[]{:S(2)}, u32[]{:S(2)}) collective-permute-start(bf16[512,512]{1,0:T(8,128)(2,1)S(1)} %collective-permute-done.1.two), channel_id=1, source_target_pairs={{0,64},{16,464},{64,128},{80,16},{128,192},{144,80},{192,256},{208... | collective-permute-start | bytes 1572872 | tf_op jit(solution)/shard_map/ppermute | solution.py:191
  32.1 0.6 copy-start.2
  34.2 12.2 %all-to-all-start.1 = ((f32[8,4,128]{2,1,0:T(4,128)}), f32[8,4,128]{2,1,0:T(4,128)S(1)}, u32[]{:S(2)}, u32[]{:S(2)}) async-start(f32[8,4,128]{2,1,0:T(4,128)} %resend.1), calls=%async_computation.1 | async-start | bytes 32768 | tf_op jit(solution)/shard_map/all_to_all | solution.py:195
  39.8 6.6 %copy-start = (bf16[1,256,512]{2,1,0:T(8,128)(2,1)S(1)}, bf16[1,256,512]{2,1,0:T(8,128)(2,1)}, u32[]{:S(2)}) copy-start(bf16[1,256,512]{2,1,0:T(8,128)(2,1)} %param.3) | copy-start | bytes 786436
  39.8 6.6 %copy-start.1 = (s32[1,2,8]{2,1,0:T(2,128)S(1)}, s32[1,2,8]{2,1,0:T(2,128)}, u32[]{:S(2)}) copy-start(s32[1,2,8]{2,1,0:T(2,128)} %bounds.3) | copy-start | bytes 196
  39.9 10.2 %collective-permute-start.4 = (bf16[256,512]{1,0:T(8,128)(2,1)S(1)}, bf16[256,512]{1,0:T(8,128)(2,1)S(1)}, u32[]{:S(2)}, u32[]{:S(2)}) collective-permute-start(bf16[256,512]{1,0:T(8,128)(2,1)S(1)} %constant_dynamic-slice_fusion), channel_id=1, source_target_pairs={{0,64},{16,464},{64,128},{80,16},{128,192},{144,80},{192,256},{208... | collective-permute-start | bytes 786440 | tf_op jit(solution)/shard_map/ppermute | solution.py:194

commit v2 on v1

--- a/solution.py
+++ b/solution.py
@@ -62,7 +62,7 @@
 
 
 def near_kernel(
-    bounds, partials, own, chip, side, two, one, unit, best, rows, cols, sems
+    bounds, partials, own, chip, side, two, one, three, unit, best, rows, cols, sems
 ):
     z, xl, core = lax.axis_index("z"), lax.axis_index("xl"), lax.axis_index("c")
     sign = 2 * core - 1
@@ -74,6 +74,7 @@
         pltpu.make_async_copy(own, cols.at[pl.ds(0, ROWS)], sems.at[2]),
         pltpu.make_async_copy(two, cols.at[pl.ds(ROWS, CHIP)], sems.at[3]),
         pltpu.make_async_copy(one, cols.at[pl.ds(ROWS + CHIP, CHIP)], sems.at[4]),
+        pltpu.make_async_copy(three, cols.at[pl.ds(ROWS + 2 * CHIP, CHIP)], sems.at[5]),
     ]
     for copy in copies:
         copy.start()
@@ -83,9 +84,9 @@
     for k in range(PLANE // STEP):
         unit[pl.ds(k * STEP, STEP)] = normalized(rows[pl.ds(k * STEP, STEP)])
     starts = [plane_start(z, xl, 0) + core * ROWS]
-    for offset in (2 * sign, sign):
+    for offset in (2 * sign, sign, 3 * sign):
         starts += [plane_start(z, xl, offset), plane_start(z, xl, offset) + ROWS]
-    waits = {0: 2, 1: 3, 3: 4}
+    waits = {0: 2, 1: 3, 3: 4, 5: 5}
     found = jnp.full((8, PLANE), NONE, jnp.float32)
     for k, start in enumerate(starts):
         if k in waits:
@@ -95,26 +96,11 @@
     best[...] = found
 
 
-def far_kernel(bounds, partials, unit, best, three, four, out, cols, sems):
+def far_kernel(bounds, partials, unit, best, four, out):
     z, xl, core = lax.axis_index("z"), lax.axis_index("xl"), lax.axis_index("c")
-    sign = 2 * core - 1
-    copies = [
-        pltpu.make_async_copy(three, cols.at[pl.ds(0, CHIP)], sems.at[0]),
-        pltpu.make_async_copy(four, cols.at[pl.ds(CHIP, ROWS)], sems.at[1]),
-    ]
-    for copy in copies:
-        copy.start()
-    normalized = normalizer(partials)
-    starts = [plane_start(z, xl, 3 * sign), plane_start(z, xl, 3 * sign) + ROWS]
-    starts += [plane_start(z, xl, 4) + core * ROWS]
-    found = best[...]
-    for k, start in enumerate(starts):
-        if k == 0:
-            copies[0].wait()
-        if k == 2:
-            copies[1].wait()
-        piece = normalized(cols[pl.ds(k * STEP, STEP)])
-        found = raise_best(found, bounds, unit, piece, start, z)
+    piece = normalizer(partials)(four[...])
+    start = plane_start(z, xl, 4) + core * ROWS
+    found = raise_best(best[...], bounds, unit, piece, start, z)
     found = jnp.max(found, axis=0, keepdims=True)
     for k in range(PLANE // 128):
         out[k // 2, pl.ds(k % 2, 1)] = found[:, k * 128 : (k + 1) * 128]
@@ -136,12 +122,12 @@
             jax.ShapeDtypeStruct((PLANE, D), jnp.bfloat16),
             jax.ShapeDtypeStruct((8, PLANE), jnp.float32),
         ),
-        in_specs=[pl.BlockSpec(memory_space=pltpu.SMEM), IN_VMEM] + [ANYWHERE] * 5,
+        in_specs=[pl.BlockSpec(memory_space=pltpu.SMEM), IN_VMEM] + [ANYWHERE] * 6,
         out_specs=(IN_VMEM, IN_VMEM),
         scratch_shapes=[
             pltpu.VMEM((PLANE, D), jnp.bfloat16),
-            pltpu.VMEM((ROWS + 2 * CHIP, D), jnp.bfloat16),
-            pltpu.SemaphoreType.DMA((5,)),
+            pltpu.VMEM((ROWS + 3 * CHIP, D), jnp.bfloat16),
+            pltpu.SemaphoreType.DMA((6,)),
         ],
         compiler_params=PARAMS,
         cost_estimate=cost(5e9),
@@ -149,20 +135,16 @@
     )(bounds, partials, *blocks)
 
 
-def far(bounds, partials, unit, best, three, four):
+def far(bounds, partials, unit, best, four):
     return pl.pallas_call(
         far_kernel,
         out_shape=jax.ShapeDtypeStruct((XL * C, ROWS // 128, 128), jnp.float32),
-        in_specs=[pl.BlockSpec(memory_space=pltpu.SMEM)] + [IN_VMEM] * 3 + [ANYWHERE] * 2,
+        in_specs=[pl.BlockSpec(memory_space=pltpu.SMEM)] + [IN_VMEM] * 4,
         out_specs=IN_VMEM,
-        scratch_shapes=[
-            pltpu.VMEM((CHIP + ROWS, D), jnp.bfloat16),
-            pltpu.SemaphoreType.DMA((2,)),
-        ],
         compiler_params=PARAMS,
         cost_estimate=cost(1e9),
         name="far",
-    )(bounds, partials, unit, best, three, four)
+    )(bounds, partials, unit, best, four)
 
 
 def resend(received, count, flops):
@@ -175,6 +157,7 @@
         out_shape=jax.ShapeDtypeStruct((count, 4, 128), jnp.float32),
         in_specs=[IN_VMEM],
         out_specs=IN_VMEM,
+        compiler_params=pltpu.CompilerParams(vmem_limit_bytes=2 * 1024 * 1024),
         cost_estimate=cost(flops),
         name="resend",
     )(received)
@@ -190,11 +173,11 @@
     sums = spread_sum(column_sums, ("z", "xl", "xh"), Z * XL * XH)
     three = lax.ppermute(two, ("z", "c"), shift((1, -1)))
     sums = resend(sums, Y, 8000000000)
-    half = lax.dynamic_slice_in_dim(three, lax.axis_index("c") * ROWS, ROWS, 0)
-    four = lax.ppermute(half, ("z", "c"), shift((1, -1)))
+    half = lax.dynamic_slice_in_dim(two, lax.axis_index("c") * ROWS, ROWS, 0)
+    four = lax.ppermute(half, ("z", "c"), shift((2, -2)))
     partials = lax.all_to_all(sums, "y", 0, 0)
-    unit, best = near(cluster_rows, partials, own, chip, side, two, one)
-    best = far(cluster_rows, partials, unit, best, three, four)
+    unit, best = near(cluster_rows, partials, own, chip, side, two, one, three)
+    best = far(cluster_rows, partials, unit, best, four)
     best = lax.all_to_all(best, ("xl", "c"), 0, 0)
     return jnp.max(best, axis=0).reshape(1, ROWS)
 

time: 62.6 us -> 61.2 us (0.978)
  Pallas kernels: 7.22 us -> 6.36 us
    pallas_call x1, Pallas kernels: 2.1 us -> 1.08 us  [far(): pl.pallas_call(far_kernel, out_shape=jax.ShapeDtypeStruct((XL * C, ROWS /...]
    pallas_call x1, Pallas kernels: 3.65 us -> 4.64 us  [near(): pl.pallas_call(near_kernel, out_shape=(jax.ShapeDtypeStruct((PLANE, D), j...]
    pallas_call x1, Pallas kernels: 1.47 us -> 0.64 us  [resend(): pl.pallas_call(kernel, out_shape=jax.ShapeDtypeStruct((count, 4, 128), jn...]
  transfers between devices with their start and end apart: 7 -> 7, of which waited for: 1 -> 1; matrix products, arithmetic and copies ran while one was open for 1% -> 1% of each run, Pallas kernels for 8% -> 9%
where the time goes in v2:
time: 61.2 us; the launch traced here: 60.8 us
  starting transfers between devices  33.2 us (54%)
  blocking collectives  18.4 us (30%)
  Pallas kernels  6.36 us (10%)
  waiting for transfers between devices  1.45 us (2%)
  other arithmetic  0.69 us (1%)
  local copies, waits for them, and re-layouts  0.68 us (1%)
    all_to_all x1, blocking collectives, on_device(): best = lax.all_to_all(best, ('xl', 'c'), 0, 0)  9.47 us
    all_gather x1, blocking collectives, on_device(): chip = lax.all_gather(own, 'c', axis=0, tiled=True)  8.89 us
    all_to_all x1, starting transfers between devices, on_device(): partials = lax.all_to_all(sums, 'y', 0, 0)  5.57 us
    all_to_all x1, starting transfers between devices, spread_sum(): lax.all_to_all(jnp.broadcast_to(partial[None], (count, 4, 128)), axes, 0, 0)  5.32 us
    ppermute x1, starting transfers between devices, on_device(): two = lax.ppermute(chip, ('z', 'c'), shift((2, -2)))  5.27 us
    ppermute x1, starting transfers between devices, on_device(): four = lax.ppermute(half, ('z', 'c'), shift((2, -2)))  5.17 us
    pallas_call x1, Pallas kernels, near(): pl.pallas_call(near_kernel, out_shape=(jax.ShapeDtypeStruct((PLANE, D), j...  4.64 us
    ppermute x1, starting transfers between devices, on_device(): one = lax.ppermute(chip, ('z', 'c'), shift((1, -1)))  4.39 us
  transfers between devices with their start and end apart: 7, of which 1 were waited for; matrix products, arithmetic and copies ran while one was open for 1% of the time, Pallas kernels for 9%

profile of v2, /device:TPU:1, one launch (start us, length us, event | category | flops | bytes accessed | tf_op | source)
XLA Modules:
  0.0 60.8 jit_solution(16690084235805081384)
XLA Ops:
  0.0 8.9 %all-gather = bf16[1,512,512]{2,1,0:T(8,128)(2,1)S(1)} all-gather(bf16[1,256,512]{2,1,0:T(8,128)(2,1)} %param.3), channel_id=2, replica_groups=mesh['z'=8,'xl'=2,'c'=2,'y'=8,'xh'=2] {'c'}, dimensions={1}, use_global_device_ids=true | all-gather | bytes 786432 | tf_op jit(solution)/shard_map/all_gather | solution.py:168
  8.9 5.3 %collective-permute-start.1 = (bf16[512,512]{1,0:T(8,128)(2,1)S(1)}, bf16[512,512]{1,0:T(8,128)(2,1)S(1)}, u32[]{:S(2)}, u32[]{:S(2)}) collective-permute-start(bf16[512,512]{1,0:T(8,128)(2,1)S(1)} %bitcast.5), channel_id=1, source_target_pairs={{0,128},{16,400},{64,192},{80,464},{128,256},{144,16},{192,320},{2... | collective-permute-start | bytes 1572872 | tf_op jit(solution)/shard_map/ppermute | solution.py:169
  14.2 0.1 convert_reduce_fusion
  14.3 0.6 %broadcast_in_dim.8 = f32[32,4,128]{2,1,0:T(4,128)} broadcast(f32[4,128]{1,0:T(4,128)S(1)} %bitcast.10), dimensions={1,2} | broadcast | bytes 67584 | tf_op jit(solution)/shard_map/broadcast_in_dim | solution.py:25
  14.9 5.3 %all-to-all-start = ((f32[32,4,128]{2,1,0:T(4,128)}), f32[32,4,128]{2,1,0:T(4,128)S(1)}, u32[]{:S(2)}, u32[]{:S(2)}) async-start(f32[32,4,128]{2,1,0:T(4,128)} %broadcast_in_dim.8), calls=%async_computation | async-start | bytes 131072 | tf_op jit(solution)/shard_map/all_to_all | solution.py:25
  20.2 3.1 %collective-permute-start = (bf16[512,512]{1,0:T(8,128)(2,1)S(1)}, bf16[512,512]{1,0:T(8,128)(2,1)S(1)}, u32[]{:S(2)}, u32[]{:S(2)}) collective-permute-start(bf16[512,512]{1,0:T(8,128)(2,1)S(1)} %bitcast.6), channel_id=1, source_target_pairs={{0,32},{32,0},{1,33},{33,1},{2,34},{34,2},{3,35},{35,3},{4,36},{36... | collective-permute-start | bytes 1572872 | tf_op jit(solution)/shard_map/ppermute | solution.py:171
  23.4 4.4 %collective-permute-start.2 = (bf16[512,512]{1,0:T(8,128)(2,1)S(1)}, bf16[512,512]{1,0:T(8,128)(2,1)S(1)}, u32[]{:S(2)}, u32[]{:S(2)}) collective-permute-start(bf16[512,512]{1,0:T(8,128)(2,1)S(1)} %bitcast.7), channel_id=1, source_target_pairs={{0,64},{16,464},{64,128},{80,16},{128,192},{144,80},{192,256},{208... | collective-permute-start | bytes 1572872 | tf_op jit(solution)/shard_map/ppermute | solution.py:170
  27.8 0.0 collective-permute-done.1.two
  27.8 4.3 %collective-permute-start.3 = (bf16[512,512]{1,0:T(8,128)(2,1)S(1)}, bf16[512,512]{1,0:T(8,128)(2,1)S(1)}, u32[]{:S(2)}, u32[]{:S(2)}) collective-permute-start(bf16[512,512]{1,0:T(8,128)(2,1)S(1)} %collective-permute-done.1.two), channel_id=1, source_target_pairs={{0,64},{16,464},{64,128},{80,16},{128,192},{144,80},{192,256},{208... | collective-permute-start | bytes 1572872 | tf_op jit(solution)/shard_map/ppermute | solution.py:174
  32.1 0.0 all-to-all-done.received
  32.1 0.6 %resend.1 = f32[8,4,128]{2,1,0:T(4,128)} custom-call(f32[32,4,128]{2,1,0:T(4,128)S(1)} %all-to-all-done.received), custom_call_target="tpu_custom_call" | custom-call | flops 8000000000 | bytes 4194304 | tf_op jit(solution)/shard_map/resend/pallas_call | solution.py:155
  32.8 5.6 %all-to-all-start.1 = ((f32[8,4,128]{2,1,0:T(4,128)}), f32[8,4,128]{2,1,0:T(4,128)S(1)}, u32[]{:S(2)}, u32[]{:S(2)}) async-start(f32[8,4,128]{2,1,0:T(4,128)} %resend.1), calls=%async_computation.1 | async-start | bytes 32768 | tf_op jit(solution)/shard_map/all_to_all | solution.py:178
  38.3 0.0 copy-start
  38.4 0.0 copy-start.1
  38.4 5.2 %collective-permute-start.4 = (bf16[256,512]{1,0:T(8,128)(2,1)S(1)}, bf16[256,512]{1,0:T(8,128)(2,1)S(1)}, u32[]{:S(2)}, u32[]{:S(2)}) collective-permute-start(bf16[256,512]{1,0:T(8,128)(2,1)S(1)} %constant_dynamic-slice_fusion), channel_id=1, source_target_pairs={{0,128},{16,400},{64,192},{80,464},{128,256},{144,16},{192,320},{2... | collective-permute-start | bytes 786440 | tf_op jit(solution)/shard_map/ppermute | solution.py:177
  43.6 1.4 %all-to-all-done.1.partials = f32[8,4,128]{2,1,0:T(4,128)S(1)} async-done(((f32[8,4,128]{2,1,0:T(4,128)}), f32[8,4,128]{2,1,0:T(4,128)S(1)}, u32[]{:S(2)}, u32[]{:S(2)}) %all-to-all-start.1) | async-done | bytes 16416 | tf_op jit(solution)/shard_map/all_to_all | solution.py:178
  45.0 0.0 collective-permute-done.side
  45.0 0.0 collective-permute-done.2.one
  45.0 0.0 collective-permute-done.3.three
  45.0 0.0 copy-done
  45.0 0.0 copy-done.1
  45.0 4.6 %near.1 = (bf16[1024,512]{1,0:T(8,128)(2,1)S(1)}, f32[8,1024]{1,0:T(8,128)S(1)}) custom-call(s32[1,2,8]{2,1,0:T(2,128)S(1)} %copy-done.1, f32[8,4,128]{2,1,0:T(4,128)S(1)} %all-to-all-done.1.partials, bf16[256,512]{1,0:T(8,128)(2,1)S(1)} %bitcast.9, bf16[512,512]{1,0:T(8,128)(2,1)S(1)} %bitcast.8, bf16[512,512]{1,0:T(8,128)(2,1)S(1)} %collective-permute-done.side, ...), custom_call_target="tpu_custom_call" | custom-call | flops 5000000000 | bytes 4194304 | tf_op jit(solution)/shard_map/near/pallas_call | solution.py:119
  49.7 0.0 collective-permute-done.4.four
  49.7 1.1 %far.1 = f32[4,2,128]{2,1,0:T(2,128)S(1)} custom-call(s32[1,2,8]{2,1,0:T(2,128)S(1)} %copy-done.1, f32[8,4,128]{2,1,0:T(4,128)S(1)} %all-to-all-done.1.partials, bf16[1024,512]{1,0:T(8,128)(2,1)S(1)} %get-tuple-element.7.unit, f32[8,1024]{1,0:T(8,128)S(1)} %get-tuple-element.8.best, bf16[256,512]{1,0:T(8,128)(2,1)S(1)} %collective-permute-done.4.four), custom_call_target="tpu_custom_call" | custom-call | flops 1000000000 | bytes 4194304 | tf_op jit(solution)/shard_map/far/pallas_call | solution.py:139
  50.8 9.5 %all_to_all.15 = f32[4,2,128]{2,1,0:T(2,128)S(1)} all-to-all(f32[4,2,128]{2,1,0:T(2,128)S(1)} %far.1), channel_id=1, replica_groups=mesh['z'=8,'xl'=2,'c'=2,'y'=8,'xh'=2] {'xl','c'}, dimensions={0} | all-to-all | bytes 8192 | tf_op jit(solution)/shard_map/all_to_all | solution.py:181
  60.3 0.6 reduce_max.9
  (1 shorter events, 0.0 us)
Async XLA Ops:
  8.9 18.9 %collective-permute-start.1 = (bf16[512,512]{1,0:T(8,128)(2,1)S(1)}, bf16[512,512]{1,0:T(8,128)(2,1)S(1)}, u32[]{:S(2)}, u32[]{:S(2)}) collective-permute-start(bf16[512,512]{1,0:T(8,128)(2,1)S(1)} %bitcast.5), channel_id=1, source_target_pairs={{0,128},{16,400},{64,192},{80,464},{128,256},{144,16},{192,320},{2... | collective-permute-start | bytes 1572872 | tf_op jit(solution)/shard_map/ppermute | solution.py:169
  14.9 17.2 %all-to-all-start = ((f32[32,4,128]{2,1,0:T(4,128)}), f32[32,4,128]{2,1,0:T(4,128)S(1)}, u32[]{:S(2)}, u32[]{:S(2)}) async-start(f32[32,4,128]{2,1,0:T(4,128)} %broadcast_in_dim.8), calls=%async_computation | async-start | bytes 131072 | tf_op jit(solution)/shard_map/all_to_all | solution.py:25
  20.2 24.7 %collective-permute-start = (bf16[512,512]{1,0:T(8,128)(2,1)S(1)}, bf16[512,512]{1,0:T(8,128)(2,1)S(1)}, u32[]{:S(2)}, u32[]{:S(2)}) collective-permute-start(bf16[512,512]{1,0:T(8,128)(2,1)S(1)} %bitcast.6), channel_id=1, source_target_pairs={{0,32},{32,0},{1,33},{33,1},{2,34},{34,2},{3,35},{35,3},{4,36},{36... | collective-permute-start | bytes 1572872 | tf_op jit(solution)/shard_map/ppermute | solution.py:171
  23.4 21.6 %collective-permute-start.2 = (bf16[512,512]{1,0:T(8,128)(2,1)S(1)}, bf16[512,512]{1,0:T(8,128)(2,1)S(1)}, u32[]{:S(2)}, u32[]{:S(2)}) collective-permute-start(bf16[512,512]{1,0:T(8,128)(2,1)S(1)} %bitcast.7), channel_id=1, source_target_pairs={{0,64},{16,464},{64,128},{80,16},{128,192},{144,80},{192,256},{208... | collective-permute-start | bytes 1572872 | tf_op jit(solution)/shard_map/ppermute | solution.py:170
  27.8 17.2 %collective-permute-start.3 = (bf16[512,512]{1,0:T(8,128)(2,1)S(1)}, bf16[512,512]{1,0:T(8,128)(2,1)S(1)}, u32[]{:S(2)}, u32[]{:S(2)}) collective-permute-start(bf16[512,512]{1,0:T(8,128)(2,1)S(1)} %collective-permute-done.1.two), channel_id=1, source_target_pairs={{0,64},{16,464},{64,128},{80,16},{128,192},{144,80},{192,256},{208... | collective-permute-start | bytes 1572872 | tf_op jit(solution)/shard_map/ppermute | solution.py:174
  32.8 12.2 %all-to-all-start.1 = ((f32[8,4,128]{2,1,0:T(4,128)}), f32[8,4,128]{2,1,0:T(4,128)S(1)}, u32[]{:S(2)}, u32[]{:S(2)}) async-start(f32[8,4,128]{2,1,0:T(4,128)} %resend.1), calls=%async_computation.1 | async-start | bytes 32768 | tf_op jit(solution)/shard_map/all_to_all | solution.py:178
  38.3 6.6 %copy-start = (bf16[1,256,512]{2,1,0:T(8,128)(2,1)S(1)}, bf16[1,256,512]{2,1,0:T(8,128)(2,1)}, u32[]{:S(2)}) copy-start(bf16[1,256,512]{2,1,0:T(8,128)(2,1)} %param.3) | copy-start | bytes 786436
  38.4 6.6 %copy-start.1 = (s32[1,2,8]{2,1,0:T(2,128)S(1)}, s32[1,2,8]{2,1,0:T(2,128)}, u32[]{:S(2)}) copy-start(s32[1,2,8]{2,1,0:T(2,128)} %bounds.3) | copy-start | bytes 196
  38.4 11.3 %collective-permute-start.4 = (bf16[256,512]{1,0:T(8,128)(2,1)S(1)}, bf16[256,512]{1,0:T(8,128)(2,1)S(1)}, u32[]{:S(2)}, u32[]{:S(2)}) collective-permute-start(bf16[256,512]{1,0:T(8,128)(2,1)S(1)} %constant_dynamic-slice_fusion), channel_id=1, source_target_pairs={{0,128},{16,400},{64,192},{80,464},{128,256},{144,16},{192,320},{2... | collective-permute-start | bytes 786440 | tf_op jit(solution)/shard_map/ppermute | solution.py:177

commit v3 on v2

--- a/solution.py
+++ b/solution.py
@@ -79,21 +79,36 @@
     for copy in copies:
         copy.start()
     normalized = normalizer(partials)
-    copies[0].wait()
-    copies[1].wait()
-    for k in range(PLANE // STEP):
-        unit[pl.ds(k * STEP, STEP)] = normalized(rows[pl.ds(k * STEP, STEP)])
     starts = [plane_start(z, xl, 0) + core * ROWS]
     for offset in (2 * sign, sign, 3 * sign):
         starts += [plane_start(z, xl, offset), plane_start(z, xl, offset) + ROWS]
     waits = {0: 2, 1: 3, 3: 4, 5: 5}
-    found = jnp.full((8, PLANE), NONE, jnp.float32)
-    for k, start in enumerate(starts):
+    for k in range(len(starts)):
         if k in waits:
             copies[waits[k]].wait()
-        piece = normalized(cols[pl.ds(k * STEP, STEP)])
-        found = raise_best(found, bounds, unit, piece, start, z, k == 0)
-    best[...] = found
+        block = pl.ds(k * STEP, STEP)
+        cols[block] = normalized(cols[block])
+    copies[0].wait()
+    copies[1].wait()
+    offset = lax.broadcasted_iota(jnp.int32, (STEP, 1), 0)
+    col_cluster = [cluster_by(bounds, start + offset) for start in starts]
+    for k in range(PLANE // STEP):
+        block = pl.ds(k * STEP, STEP)
+        slab = normalized(rows[block])
+        unit[block] = slab
+        position = z * PLANE + k * STEP + lax.broadcasted_iota(jnp.int32, (1, STEP), 1)
+        row_cluster = cluster_by(bounds, position)
+        scores = lax.dot_general(
+            cols[...], slab, (((1,), (1,)), ((), ())), preferred_element_type=jnp.float32
+        )
+        found = jnp.full((8, STEP), NONE, jnp.float32)
+        for j, start in enumerate(starts):
+            inside = col_cluster[j] == row_cluster
+            if j == 0:
+                inside &= start + offset != position
+            part = jnp.where(inside, scores[j * STEP : (j + 1) * STEP], NONE)
+            found = jnp.maximum(found, jnp.max(part.reshape(STEP // 8, 8, STEP), axis=0))
+        best[:, block] = found
 
 
 def far_kernel(bounds, partials, unit, best, four, out):
@@ -170,12 +185,12 @@
     one = lax.ppermute(chip, ("z", "c"), shift((1, -1)))
     side = lax.ppermute(chip, "xl", [(0, 1), (1, 0)])
     column_sums = jnp.sum(chip, axis=0, dtype=jnp.float32).reshape(4, 128)
-    sums = spread_sum(column_sums, ("z", "xl", "xh"), Z * XL * XH)
+    sums = spread_sum(column_sums, ("xl", "y", "xh"), XL * Y * XH)
     three = lax.ppermute(two, ("z", "c"), shift((1, -1)))
-    sums = resend(sums, Y, 8000000000)
+    sums = resend(sums, Z, 8000000000)
     half = lax.dynamic_slice_in_dim(two, lax.axis_index("c") * ROWS, ROWS, 0)
     four = lax.ppermute(half, ("z", "c"), shift((2, -2)))
-    partials = lax.all_to_all(sums, "y", 0, 0)
+    partials = lax.all_to_all(sums, "z", 0, 0)
     unit, best = near(cluster_rows, partials, own, chip, side, two, one, three)
     best = far(cluster_rows, partials, unit, best, four)
     best = lax.all_to_all(best, ("xl", "c"), 0, 0)

time: 61.2 us -> 60.2 us (0.984)
  waiting for transfers between devices: 1.45 us -> 5.12 us
  blocking collectives: 18.4 us -> 15.5 us
  starting transfers between devices: 33.2 us -> 31.3 us
    all_to_all x1, starting transfers between devices: 5.32 us -> 9.67 us  [spread_sum(): lax.all_to_all(jnp.broadcast_to(partial[None], (count, 4, 128)), axes, 0, 0)]
    all_to_all x1, blocking collectives: 9.47 us -> 6.66 us  [on_device(): best = lax.all_to_all(best, ('xl', 'c'), 0, 0)]
    all_to_all x1, starting transfers between devices: 5.57 us -> 3.33 us  [on_device(): partials = lax.all_to_all(sums, 'z', 0, 0)]
    ppermute x1, starting transfers between devices: 4.39 us -> 2.18 us  [on_device(): one = lax.ppermute(chip, ('z', 'c'), shift((1, -1)))]
    all_to_all x1, waiting for transfers between devices: 1.4 us -> 3.55 us  [on_device(): partials = lax.all_to_all(sums, 'z', 0, 0)]
    ppermute x1, starting transfers between devices: 4.31 us -> 2.18 us  [on_device(): three = lax.ppermute(two, ('z', 'c'), shift((1, -1)))]
    all_to_all x1, waiting for transfers between devices: 0.01 us -> 1.56 us  [spread_sum(): lax.all_to_all(jnp.broadcast_to(partial[None], (count, 4, 128)), axes, 0, 0)]
  transfers between devices with their start and end apart: 7 -> 7, of which waited for: 1 -> 2; matrix products, arithmetic and copies ran while one was open for 1% -> 1% of each run, Pallas kernels for 9% -> 9%
where the time goes in v3:
time: 60.2 us; the launch traced here: 59.8 us
  starting transfers between devices  31.3 us (52%)
  blocking collectives  15.5 us (26%)
  Pallas kernels  6.28 us (10%)
  waiting for transfers between devices  5.12 us (9%)
  other arithmetic  0.69 us (1%)
  local copies, waits for them, and re-layouts  0.68 us (1%)
    all_to_all x1, starting transfers between devices, spread_sum(): lax.all_to_all(jnp.broadcast_to(partial[None], (count, 4, 128)), axes, 0, 0)  9.67 us
    all_gather x1, blocking collectives, on_device(): chip = lax.all_gather(own, 'c', axis=0, tiled=True)  8.89 us
    all_to_all x1, blocking collectives, on_device(): best = lax.all_to_all(best, ('xl', 'c'), 0, 0)  6.66 us
    ppermute x1, starting transfers between devices, on_device(): four = lax.ppermute(half, ('z', 'c'), shift((2, -2)))  5.52 us
    ppermute x1, starting transfers between devices, on_device(): two = lax.ppermute(chip, ('z', 'c'), shift((2, -2)))  5.27 us
    pallas_call x1, Pallas kernels, near(): pl.pallas_call(near_kernel, out_shape=(jax.ShapeDtypeStruct((PLANE, D), j...  4.55 us
    all_to_all x1, waiting for transfers between devices, on_device(): partials = lax.all_to_all(sums, 'z', 0, 0)  3.55 us
    all_to_all x1, starting transfers between devices, on_device(): partials = lax.all_to_all(sums, 'z', 0, 0)  3.33 us
  transfers between devices with their start and end apart: 7, of which 2 were waited for; matrix products, arithmetic and copies ran while one was open for 1% of the time, Pallas kernels for 9%

profile of v3, /device:TPU:1, one launch (start us, length us, event | category | flops | bytes accessed | tf_op | source)
XLA Modules:
  0.0 59.8 jit_solution(9974586244159897745)
XLA Ops:
  0.0 8.9 %all-gather = bf16[1,512,512]{2,1,0:T(8,128)(2,1)S(1)} all-gather(bf16[1,256,512]{2,1,0:T(8,128)(2,1)} %param.3), channel_id=2, replica_groups=mesh['z'=8,'xl'=2,'c'=2,'y'=8,'xh'=2] {'c'}, dimensions={1}, use_global_device_ids=true | all-gather | bytes 786432 | tf_op jit(solution)/shard_map/all_gather | solution.py:183
  8.9 5.3 %collective-permute-start.1 = (bf16[512,512]{1,0:T(8,128)(2,1)S(1)}, bf16[512,512]{1,0:T(8,128)(2,1)S(1)}, u32[]{:S(2)}, u32[]{:S(2)}) collective-permute-start(bf16[512,512]{1,0:T(8,128)(2,1)S(1)} %bitcast.5), channel_id=1, source_target_pairs={{0,128},{16,400},{64,192},{80,464},{128,256},{144,16},{192,320},{2... | collective-permute-start | bytes 1572872 | tf_op jit(solution)/shard_map/ppermute | solution.py:184
  14.2 0.1 convert_reduce_fusion
  14.3 0.6 %broadcast_in_dim.8 = f32[32,4,128]{2,1,0:T(4,128)} broadcast(f32[4,128]{1,0:T(4,128)S(1)} %bitcast.10), dimensions={1,2} | broadcast | bytes 67584 | tf_op jit(solution)/shard_map/broadcast_in_dim | solution.py:25
  14.9 9.7 %all-to-all-start = ((f32[32,4,128]{2,1,0:T(4,128)}), f32[32,4,128]{2,1,0:T(4,128)S(1)}, u32[]{:S(2)}, u32[]{:S(2)}) async-start(f32[32,4,128]{2,1,0:T(4,128)} %broadcast_in_dim.8), calls=%async_computation | async-start | bytes 131072 | tf_op jit(solution)/shard_map/all_to_all | solution.py:25
  24.6 3.1 %collective-permute-start = (bf16[512,512]{1,0:T(8,128)(2,1)S(1)}, bf16[512,512]{1,0:T(8,128)(2,1)S(1)}, u32[]{:S(2)}, u32[]{:S(2)}) collective-permute-start(bf16[512,512]{1,0:T(8,128)(2,1)S(1)} %bitcast.6), channel_id=1, source_target_pairs={{0,32},{32,0},{1,33},{33,1},{2,34},{34,2},{3,35},{35,3},{4,36},{36... | collective-permute-start | bytes 1572872 | tf_op jit(solution)/shard_map/ppermute | solution.py:186
  27.8 2.2 %collective-permute-start.2 = (bf16[512,512]{1,0:T(8,128)(2,1)S(1)}, bf16[512,512]{1,0:T(8,128)(2,1)S(1)}, u32[]{:S(2)}, u32[]{:S(2)}) collective-permute-start(bf16[512,512]{1,0:T(8,128)(2,1)S(1)} %bitcast.7), channel_id=1, source_target_pairs={{0,64},{16,464},{64,128},{80,16},{128,192},{144,80},{192,256},{208... | collective-permute-start | bytes 1572872 | tf_op jit(solution)/shard_map/ppermute | solution.py:185
  29.9 0.0 collective-permute-done.1.two
  30.0 2.2 %collective-permute-start.3 = (bf16[512,512]{1,0:T(8,128)(2,1)S(1)}, bf16[512,512]{1,0:T(8,128)(2,1)S(1)}, u32[]{:S(2)}, u32[]{:S(2)}) collective-permute-start(bf16[512,512]{1,0:T(8,128)(2,1)S(1)} %collective-permute-done.1.two), channel_id=1, source_target_pairs={{0,64},{16,464},{64,128},{80,16},{128,192},{144,80},{192,256},{208... | collective-permute-start | bytes 1572872 | tf_op jit(solution)/shard_map/ppermute | solution.py:189
  32.1 1.6 %all-to-all-done.received = f32[32,4,128]{2,1,0:T(4,128)S(1)} async-done(((f32[32,4,128]{2,1,0:T(4,128)}), f32[32,4,128]{2,1,0:T(4,128)S(1)}, u32[]{:S(2)}, u32[]{:S(2)}) %all-to-all-start) | async-done | bytes 65568 | tf_op jit(solution)/shard_map/all_to_all | solution.py:25
  33.7 0.6 %resend.1 = f32[8,4,128]{2,1,0:T(4,128)} custom-call(f32[32,4,128]{2,1,0:T(4,128)S(1)} %all-to-all-done.received), custom_call_target="tpu_custom_call" | custom-call | flops 8000000000 | bytes 4194304 | tf_op jit(solution)/shard_map/resend/pallas_call | solution.py:170
  34.3 3.3 %all-to-all-start.1 = ((f32[8,4,128]{2,1,0:T(4,128)}), f32[8,4,128]{2,1,0:T(4,128)S(1)}, u32[]{:S(2)}, u32[]{:S(2)}) async-start(f32[8,4,128]{2,1,0:T(4,128)} %resend.1), calls=%async_computation.1 | async-start | bytes 32768 | tf_op jit(solution)/shard_map/all_to_all | solution.py:193
  37.7 0.0 copy-start
  37.7 0.0 copy-start.1
  37.7 5.5 %collective-permute-start.4 = (bf16[256,512]{1,0:T(8,128)(2,1)S(1)}, bf16[256,512]{1,0:T(8,128)(2,1)S(1)}, u32[]{:S(2)}, u32[]{:S(2)}) collective-permute-start(bf16[256,512]{1,0:T(8,128)(2,1)S(1)} %constant_dynamic-slice_fusion), channel_id=1, source_target_pairs={{0,128},{16,400},{64,192},{80,464},{128,256},{144,16},{192,320},{2... | collective-permute-start | bytes 786440 | tf_op jit(solution)/shard_map/ppermute | solution.py:192
  43.3 3.6 %all-to-all-done.1.partials = f32[8,4,128]{2,1,0:T(4,128)S(1)} async-done(((f32[8,4,128]{2,1,0:T(4,128)}), f32[8,4,128]{2,1,0:T(4,128)S(1)}, u32[]{:S(2)}, u32[]{:S(2)}) %all-to-all-start.1) | async-done | bytes 16416 | tf_op jit(solution)/shard_map/all_to_all | solution.py:193
  46.8 0.0 collective-permute-done.side
  46.8 0.0 collective-permute-done.2.one
  46.8 0.0 collective-permute-done.3.three
  46.8 0.0 copy-done
  46.9 0.0 copy-done.1
  46.9 4.6 %near.1 = (bf16[1024,512]{1,0:T(8,128)(2,1)S(1)}, f32[8,1024]{1,0:T(8,128)S(1)}) custom-call(s32[1,2,8]{2,1,0:T(2,128)S(1)} %copy-done.1, f32[8,4,128]{2,1,0:T(4,128)S(1)} %all-to-all-done.1.partials, bf16[256,512]{1,0:T(8,128)(2,1)S(1)} %bitcast.9, bf16[512,512]{1,0:T(8,128)(2,1)S(1)} %bitcast.8, bf16[512,512]{1,0:T(8,128)(2,1)S(1)} %collective-permute-done.side, ...), custom_call_target="tpu_custom_call" | custom-call | flops 5000000000 | bytes 4194304 | tf_op jit(solution)/shard_map/near/pallas_call | solution.py:134
  51.4 0.0 collective-permute-done.4.four
  51.4 1.1 %far.1 = f32[4,2,128]{2,1,0:T(2,128)S(1)} custom-call(s32[1,2,8]{2,1,0:T(2,128)S(1)} %copy-done.1, f32[8,4,128]{2,1,0:T(4,128)S(1)} %all-to-all-done.1.partials, bf16[1024,512]{1,0:T(8,128)(2,1)S(1)} %get-tuple-element.7.unit, f32[8,1024]{1,0:T(8,128)S(1)} %get-tuple-element.8.best, bf16[256,512]{1,0:T(8,128)(2,1)S(1)} %collective-permute-done.4.four), custom_call_target="tpu_custom_call" | custom-call | flops 1000000000 | bytes 4194304 | tf_op jit(solution)/shard_map/far/pallas_call | solution.py:154
  52.5 6.7 %all_to_all.15 = f32[4,2,128]{2,1,0:T(2,128)S(1)} all-to-all(f32[4,2,128]{2,1,0:T(2,128)S(1)} %far.1), channel_id=1, replica_groups=mesh['z'=8,'xl'=2,'c'=2,'y'=8,'xh'=2] {'xl','c'}, dimensions={0} | all-to-all | bytes 8192 | tf_op jit(solution)/shard_map/all_to_all | solution.py:196
  59.2 0.6 reduce_max.9
  (1 shorter events, 0.0 us)
Async XLA Ops:
  8.9 21.1 %collective-permute-start.1 = (bf16[512,512]{1,0:T(8,128)(2,1)S(1)}, bf16[512,512]{1,0:T(8,128)(2,1)S(1)}, u32[]{:S(2)}, u32[]{:S(2)}) collective-permute-start(bf16[512,512]{1,0:T(8,128)(2,1)S(1)} %bitcast.5), channel_id=1, source_target_pairs={{0,128},{16,400},{64,192},{80,464},{128,256},{144,16},{192,320},{2... | collective-permute-start | bytes 1572872 | tf_op jit(solution)/shard_map/ppermute | solution.py:184
  14.9 18.8 %all-to-all-start = ((f32[32,4,128]{2,1,0:T(4,128)}), f32[32,4,128]{2,1,0:T(4,128)S(1)}, u32[]{:S(2)}, u32[]{:S(2)}) async-start(f32[32,4,128]{2,1,0:T(4,128)} %broadcast_in_dim.8), calls=%async_computation | async-start | bytes 131072 | tf_op jit(solution)/shard_map/all_to_all | solution.py:25
  24.6 22.2 %collective-permute-start = (bf16[512,512]{1,0:T(8,128)(2,1)S(1)}, bf16[512,512]{1,0:T(8,128)(2,1)S(1)}, u32[]{:S(2)}, u32[]{:S(2)}) collective-permute-start(bf16[512,512]{1,0:T(8,128)(2,1)S(1)} %bitcast.6), channel_id=1, source_target_pairs={{0,32},{32,0},{1,33},{33,1},{2,34},{34,2},{3,35},{35,3},{4,36},{36... | collective-permute-start | bytes 1572872 | tf_op jit(solution)/shard_map/ppermute | solution.py:186
  27.8 19.1 %collective-permute-start.2 = (bf16[512,512]{1,0:T(8,128)(2,1)S(1)}, bf16[512,512]{1,0:T(8,128)(2,1)S(1)}, u32[]{:S(2)}, u32[]{:S(2)}) collective-permute-start(bf16[512,512]{1,0:T(8,128)(2,1)S(1)} %bitcast.7), channel_id=1, source_target_pairs={{0,64},{16,464},{64,128},{80,16},{128,192},{144,80},{192,256},{208... | collective-permute-start | bytes 1572872 | tf_op jit(solution)/shard_map/ppermute | solution.py:185
  30.0 16.9 %collective-permute-start.3 = (bf16[512,512]{1,0:T(8,128)(2,1)S(1)}, bf16[512,512]{1,0:T(8,128)(2,1)S(1)}, u32[]{:S(2)}, u32[]{:S(2)}) collective-permute-start(bf16[512,512]{1,0:T(8,128)(2,1)S(1)} %collective-permute-done.1.two), channel_id=1, source_target_pairs={{0,64},{16,464},{64,128},{80,16},{128,192},{144,80},{192,256},{208... | collective-permute-start | bytes 1572872 | tf_op jit(solution)/shard_map/ppermute | solution.py:189
  34.3 12.5 %all-to-all-start.1 = ((f32[8,4,128]{2,1,0:T(4,128)}), f32[8,4,128]{2,1,0:T(4,128)S(1)}, u32[]{:S(2)}, u32[]{:S(2)}) async-start(f32[8,4,128]{2,1,0:T(4,128)} %resend.1), calls=%async_computation.1 | async-start | bytes 32768 | tf_op jit(solution)/shard_map/all_to_all | solution.py:193
  37.7 9.2 %copy-start = (bf16[1,256,512]{2,1,0:T(8,128)(2,1)S(1)}, bf16[1,256,512]{2,1,0:T(8,128)(2,1)}, u32[]{:S(2)}) copy-start(bf16[1,256,512]{2,1,0:T(8,128)(2,1)} %param.3) | copy-start | bytes 786436
  37.7 9.1 %copy-start.1 = (s32[1,2,8]{2,1,0:T(2,128)S(1)}, s32[1,2,8]{2,1,0:T(2,128)}, u32[]{:S(2)}) copy-start(s32[1,2,8]{2,1,0:T(2,128)} %bounds.3) | copy-start | bytes 196
  37.7 13.7 %collective-permute-start.4 = (bf16[256,512]{1,0:T(8,128)(2,1)S(1)}, bf16[256,512]{1,0:T(8,128)(2,1)S(1)}, u32[]{:S(2)}, u32[]{:S(2)}) collective-permute-start(bf16[256,512]{1,0:T(8,128)(2,1)S(1)} %constant_dynamic-slice_fusion), channel_id=1, source_target_pairs={{0,128},{16,400},{64,192},{80,464},{128,256},{144,16},{192,320},{2... | collective-permute-start | bytes 786440 | tf_op jit(solution)/shard_map/ppermute | solution.py:192

commit v4 on v3

--- a/solution.py
+++ b/solution.py
@@ -48,64 +48,38 @@
     return member
 
 
-def raise_best(best, bounds, unit, piece, start, z, diagonal=False):
-    row_position = z * PLANE + lax.broadcasted_iota(jnp.int32, (1, PLANE), 1)
-    scores = lax.dot_general(
-        piece, unit[...], (((1,), (1,)), ((), ())), preferred_element_type=jnp.float32
-    )
-    position = start + lax.broadcasted_iota(jnp.int32, (STEP, 1), 0)
-    inside = cluster_by(bounds, position) == cluster_by(bounds, row_position)
-    if diagonal:
-        inside &= position != row_position
-    scores = jnp.where(inside, scores, NONE)
-    return jnp.maximum(best, jnp.max(scores.reshape(STEP // 8, 8, PLANE), axis=0))
+def row_positions(z, xl):
+    lane = lax.broadcasted_iota(jnp.int32, (1, PLANE), 1)
+    return z * PLANE + jnp.where(lane < CHIP, xl * CHIP + lane, lane - xl * CHIP)
 
 
-def near_kernel(
-    bounds, partials, own, chip, side, two, one, three, unit, best, rows, cols, sems
-):
+def near_kernel(bounds, partials, own, chip, side, two, one, three, unit, best, cols):
     z, xl, core = lax.axis_index("z"), lax.axis_index("xl"), lax.axis_index("c")
     sign = 2 * core - 1
-    here = pl.multiple_of(xl * CHIP, CHIP)
-    there = pl.multiple_of((1 - xl) * CHIP, CHIP)
-    copies = [
-        pltpu.make_async_copy(chip, rows.at[pl.ds(here, CHIP)], sems.at[0]),
-        pltpu.make_async_copy(side, rows.at[pl.ds(there, CHIP)], sems.at[1]),
-        pltpu.make_async_copy(own, cols.at[pl.ds(0, ROWS)], sems.at[2]),
-        pltpu.make_async_copy(two, cols.at[pl.ds(ROWS, CHIP)], sems.at[3]),
-        pltpu.make_async_copy(one, cols.at[pl.ds(ROWS + CHIP, CHIP)], sems.at[4]),
-        pltpu.make_async_copy(three, cols.at[pl.ds(ROWS + 2 * CHIP, CHIP)], sems.at[5]),
-    ]
-    for copy in copies:
-        copy.start()
     normalized = normalizer(partials)
     starts = [plane_start(z, xl, 0) + core * ROWS]
-    for offset in (2 * sign, sign, 3 * sign):
-        starts += [plane_start(z, xl, offset), plane_start(z, xl, offset) + ROWS]
-    waits = {0: 2, 1: 3, 3: 4, 5: 5}
-    for k in range(len(starts)):
-        if k in waits:
-            copies[waits[k]].wait()
-        block = pl.ds(k * STEP, STEP)
-        cols[block] = normalized(cols[block])
-    copies[0].wait()
-    copies[1].wait()
+    cols[pl.ds(0, ROWS)] = normalized(own[...])
+    for block, hops in ((two, 2), (one, 1), (three, 3)):
+        for k in range(CHIP // STEP):
+            cols[pl.ds(len(starts) * STEP, STEP)] = normalized(block[pl.ds(k * STEP, STEP)])
+            starts.append(plane_start(z, xl, hops * sign) + k * STEP)
     offset = lax.broadcasted_iota(jnp.int32, (STEP, 1), 0)
     col_cluster = [cluster_by(bounds, start + offset) for start in starts]
+    rows = row_positions(z, xl)
+    row_cluster = cluster_by(bounds, rows)
     for k in range(PLANE // STEP):
         block = pl.ds(k * STEP, STEP)
-        slab = normalized(rows[block])
+        source = chip if k < CHIP // STEP else side
+        slab = normalized(source[pl.ds(k * STEP % CHIP, STEP)])
         unit[block] = slab
-        position = z * PLANE + k * STEP + lax.broadcasted_iota(jnp.int32, (1, STEP), 1)
-        row_cluster = cluster_by(bounds, position)
         scores = lax.dot_general(
             cols[...], slab, (((1,), (1,)), ((), ())), preferred_element_type=jnp.float32
         )
         found = jnp.full((8, STEP), NONE, jnp.float32)
         for j, start in enumerate(starts):
-            inside = col_cluster[j] == row_cluster
+            inside = col_cluster[j] == row_cluster[:, k * STEP : (k + 1) * STEP]
             if j == 0:
-                inside &= start + offset != position
+                inside &= start + offset != rows[:, k * STEP : (k + 1) * STEP]
             part = jnp.where(inside, scores[j * STEP : (j + 1) * STEP], NONE)
             found = jnp.maximum(found, jnp.max(part.reshape(STEP // 8, 8, STEP), axis=0))
         best[:, block] = found
@@ -114,15 +88,21 @@
 def far_kernel(bounds, partials, unit, best, four, out):
     z, xl, core = lax.axis_index("z"), lax.axis_index("xl"), lax.axis_index("c")
     piece = normalizer(partials)(four[...])
+    scores = lax.dot_general(
+        piece, unit[...], (((1,), (1,)), ((), ())), preferred_element_type=jnp.float32
+    )
     start = plane_start(z, xl, 4) + core * ROWS
-    found = raise_best(best[...], bounds, unit, piece, start, z)
+    position = start + lax.broadcasted_iota(jnp.int32, (STEP, 1), 0)
+    inside = cluster_by(bounds, position) == cluster_by(bounds, row_positions(z, xl))
+    scores = jnp.where(inside, scores, NONE)
+    found = jnp.maximum(best[...], jnp.max(scores.reshape(STEP // 8, 8, PLANE), axis=0))
     found = jnp.max(found, axis=0, keepdims=True)
     for k in range(PLANE // 128):
-        out[k // 2, pl.ds(k % 2, 1)] = found[:, k * 128 : (k + 1) * 128]
+        device = lax.rem(2 * xl + k // 2, 4)
+        out[device, pl.ds(k % 2, 1)] = found[:, k * 128 : (k + 1) * 128]
 
 
 IN_VMEM = pl.BlockSpec(memory_space=pltpu.VMEM)
-ANYWHERE = pl.BlockSpec(memory_space=pl.ANY)
 PARAMS = pltpu.CompilerParams(vmem_limit_bytes=32 * 1024 * 1024)
 
 
@@ -137,13 +117,9 @@
             jax.ShapeDtypeStruct((PLANE, D), jnp.bfloat16),
             jax.ShapeDtypeStruct((8, PLANE), jnp.float32),
         ),
-        in_specs=[pl.BlockSpec(memory_space=pltpu.SMEM), IN_VMEM] + [ANYWHERE] * 6,
+        in_specs=[pl.BlockSpec(memory_space=pltpu.SMEM)] + [IN_VMEM] * (1 + len(blocks)),
         out_specs=(IN_VMEM, IN_VMEM),
-        scratch_shapes=[
-            pltpu.VMEM((PLANE, D), jnp.bfloat16),
-            pltpu.VMEM((ROWS + 3 * CHIP, D), jnp.bfloat16),
-            pltpu.SemaphoreType.DMA((6,)),
-        ],
+        scratch_shapes=[pltpu.VMEM((ROWS + 3 * CHIP, D), jnp.bfloat16)],
         compiler_params=PARAMS,
         cost_estimate=cost(5e9),
         name="near",

time: 60.2 us -> 59.3 us (0.985)
  Pallas kernels: 6.28 us -> 5.39 us
    pallas_call x1, Pallas kernels: 4.55 us -> 3.68 us  [near(): pl.pallas_call(near_kernel, out_shape=(jax.ShapeDtypeStruct((PLANE, D), j...]
  transfers between devices with their start and end apart: 7 -> 7, of which waited for: 2 -> 2; matrix products, arithmetic and copies ran while one was open for 1% -> 1% of each run, Pallas kernels for 9% -> 7%
where the time goes in v4:
time: 59.3 us; the launch traced here: 58.9 us
  starting transfers between devices  31.3 us (53%)
  blocking collectives  15.6 us (26%)
  Pallas kernels  5.39 us (9%)
  waiting for transfers between devices  5.12 us (9%)
  other arithmetic  0.69 us (1%)
  local copies, waits for them, and re-layouts  0.68 us (1%)
    all_to_all x1, starting transfers between devices, spread_sum(): lax.all_to_all(jnp.broadcast_to(partial[None], (count, 4, 128)), axes, 0, 0)  9.67 us
    all_gather x1, blocking collectives, on_device(): chip = lax.all_gather(own, 'c', axis=0, tiled=True)  8.89 us
    all_to_all x1, blocking collectives, on_device(): best = lax.all_to_all(best, ('xl', 'c'), 0, 0)  6.67 us
    ppermute x1, starting transfers between devices, on_device(): four = lax.ppermute(half, ('z', 'c'), shift((2, -2)))  5.52 us
    ppermute x1, starting transfers between devices, on_device(): two = lax.ppermute(chip, ('z', 'c'), shift((2, -2)))  5.27 us
    pallas_call x1, Pallas kernels, near(): pl.pallas_call(near_kernel, out_shape=(jax.ShapeDtypeStruct((PLANE, D), j...  3.68 us
    all_to_all x1, waiting for transfers between devices, on_device(): partials = lax.all_to_all(sums, 'z', 0, 0)  3.55 us
    all_to_all x1, starting transfers between devices, on_device(): partials = lax.all_to_all(sums, 'z', 0, 0)  3.33 us
  transfers between devices with their start and end apart: 7, of which 2 were waited for; matrix products, arithmetic and copies ran while one was open for 1% of the time, Pallas kernels for 7%

profile of v4, /device:TPU:1, one launch (start us, length us, event | category | flops | bytes accessed | tf_op | source)
XLA Modules:
  0.0 58.9 jit_solution(17366780718322242104)
XLA Ops:
  0.0 8.9 %all-gather = bf16[1,512,512]{2,1,0:T(8,128)(2,1)S(1)} all-gather(bf16[1,256,512]{2,1,0:T(8,128)(2,1)} %param.3), channel_id=2, replica_groups=mesh['z'=8,'xl'=2,'c'=2,'y'=8,'xh'=2] {'c'}, dimensions={1}, use_global_device_ids=true | all-gather | bytes 786432 | tf_op jit(solution)/shard_map/all_gather | solution.py:159
  8.9 5.3 %collective-permute-start.1 = (bf16[512,512]{1,0:T(8,128)(2,1)S(1)}, bf16[512,512]{1,0:T(8,128)(2,1)S(1)}, u32[]{:S(2)}, u32[]{:S(2)}) collective-permute-start(bf16[512,512]{1,0:T(8,128)(2,1)S(1)} %bitcast.5), channel_id=1, source_target_pairs={{0,128},{16,400},{64,192},{80,464},{128,256},{144,16},{192,320},{2... | collective-permute-start | bytes 1572872 | tf_op jit(solution)/shard_map/ppermute | solution.py:160
  14.2 0.1 convert_reduce_fusion
  14.3 0.6 %broadcast_in_dim.8 = f32[32,4,128]{2,1,0:T(4,128)} broadcast(f32[4,128]{1,0:T(4,128)S(1)} %bitcast.10), dimensions={1,2} | broadcast | bytes 67584 | tf_op jit(solution)/shard_map/broadcast_in_dim | solution.py:25
  14.9 9.7 %all-to-all-start = ((f32[32,4,128]{2,1,0:T(4,128)}), f32[32,4,128]{2,1,0:T(4,128)S(1)}, u32[]{:S(2)}, u32[]{:S(2)}) async-start(f32[32,4,128]{2,1,0:T(4,128)} %broadcast_in_dim.8), calls=%async_computation | async-start | bytes 131072 | tf_op jit(solution)/shard_map/all_to_all | solution.py:25
  24.6 3.1 %collective-permute-start = (bf16[512,512]{1,0:T(8,128)(2,1)S(1)}, bf16[512,512]{1,0:T(8,128)(2,1)S(1)}, u32[]{:S(2)}, u32[]{:S(2)}) collective-permute-start(bf16[512,512]{1,0:T(8,128)(2,1)S(1)} %bitcast.6), channel_id=1, source_target_pairs={{0,32},{32,0},{1,33},{33,1},{2,34},{34,2},{3,35},{35,3},{4,36},{36... | collective-permute-start | bytes 1572872 | tf_op jit(solution)/shard_map/ppermute | solution.py:162
  27.8 2.2 %collective-permute-start.2 = (bf16[512,512]{1,0:T(8,128)(2,1)S(1)}, bf16[512,512]{1,0:T(8,128)(2,1)S(1)}, u32[]{:S(2)}, u32[]{:S(2)}) collective-permute-start(bf16[512,512]{1,0:T(8,128)(2,1)S(1)} %bitcast.7), channel_id=1, source_target_pairs={{0,64},{16,464},{64,128},{80,16},{128,192},{144,80},{192,256},{208... | collective-permute-start | bytes 1572872 | tf_op jit(solution)/shard_map/ppermute | solution.py:161
  29.9 0.0 collective-permute-done.1.two
  30.0 2.2 %collective-permute-start.3 = (bf16[512,512]{1,0:T(8,128)(2,1)S(1)}, bf16[512,512]{1,0:T(8,128)(2,1)S(1)}, u32[]{:S(2)}, u32[]{:S(2)}) collective-permute-start(bf16[512,512]{1,0:T(8,128)(2,1)S(1)} %collective-permute-done.1.two), channel_id=1, source_target_pairs={{0,64},{16,464},{64,128},{80,16},{128,192},{144,80},{192,256},{208... | collective-permute-start | bytes 1572872 | tf_op jit(solution)/shard_map/ppermute | solution.py:165
  32.1 1.6 %all-to-all-done.received = f32[32,4,128]{2,1,0:T(4,128)S(1)} async-done(((f32[32,4,128]{2,1,0:T(4,128)}), f32[32,4,128]{2,1,0:T(4,128)S(1)}, u32[]{:S(2)}, u32[]{:S(2)}) %all-to-all-start) | async-done | bytes 65568 | tf_op jit(solution)/shard_map/all_to_all | solution.py:25
  33.7 0.6 %resend.1 = f32[8,4,128]{2,1,0:T(4,128)} custom-call(f32[32,4,128]{2,1,0:T(4,128)S(1)} %all-to-all-done.received), custom_call_target="tpu_custom_call" | custom-call | flops 8000000000 | bytes 4194304 | tf_op jit(solution)/shard_map/resend/pallas_call | solution.py:146
  34.3 3.3 %all-to-all-start.1 = ((f32[8,4,128]{2,1,0:T(4,128)}), f32[8,4,128]{2,1,0:T(4,128)S(1)}, u32[]{:S(2)}, u32[]{:S(2)}) async-start(f32[8,4,128]{2,1,0:T(4,128)} %resend.1), calls=%async_computation.1 | async-start | bytes 32768 | tf_op jit(solution)/shard_map/all_to_all | solution.py:169
  37.7 0.0 copy-start
  37.7 0.0 copy-start.1
  37.7 5.5 %collective-permute-start.4 = (bf16[256,512]{1,0:T(8,128)(2,1)S(1)}, bf16[256,512]{1,0:T(8,128)(2,1)S(1)}, u32[]{:S(2)}, u32[]{:S(2)}) collective-permute-start(bf16[256,512]{1,0:T(8,128)(2,1)S(1)} %constant_dynamic-slice_fusion), channel_id=1, source_target_pairs={{0,128},{16,400},{64,192},{80,464},{128,256},{144,16},{192,320},{2... | collective-permute-start | bytes 786440 | tf_op jit(solution)/shard_map/ppermute | solution.py:168
  43.3 3.6 %all-to-all-done.1.partials = f32[8,4,128]{2,1,0:T(4,128)S(1)} async-done(((f32[8,4,128]{2,1,0:T(4,128)}), f32[8,4,128]{2,1,0:T(4,128)S(1)}, u32[]{:S(2)}, u32[]{:S(2)}) %all-to-all-start.1) | async-done | bytes 16416 | tf_op jit(solution)/shard_map/all_to_all | solution.py:169
  46.8 0.0 collective-permute-done.side
  46.8 0.0 collective-permute-done.2.one
  46.8 0.0 collective-permute-done.3.three
  46.8 0.0 copy-done
  46.9 0.0 copy-done.1
  46.9 3.7 %near.1 = (bf16[1024,512]{1,0:T(8,128)(2,1)S(1)}, f32[8,1024]{1,0:T(8,128)S(1)}) custom-call(s32[1,2,8]{2,1,0:T(2,128)S(1)} %copy-done.1, f32[8,4,128]{2,1,0:T(4,128)S(1)} %all-to-all-done.1.partials, bf16[256,512]{1,0:T(8,128)(2,1)S(1)} %bitcast.9, bf16[512,512]{1,0:T(8,128)(2,1)S(1)} %bitcast.8, bf16[512,512]{1,0:T(8,128)(2,1)S(1)} %collective-permute-done.side, ...), custom_call_target="tpu_custom_call" | custom-call | flops 5000000000 | bytes 4194304 | tf_op jit(solution)/shard_map/near/pallas_call | solution.py:114
  50.5 0.0 collective-permute-done.4.four
  50.6 1.1 %far.1 = f32[4,2,128]{2,1,0:T(2,128)S(1)} custom-call(s32[1,2,8]{2,1,0:T(2,128)S(1)} %copy-done.1, f32[8,4,128]{2,1,0:T(4,128)S(1)} %all-to-all-done.1.partials, bf16[1024,512]{1,0:T(8,128)(2,1)S(1)} %get-tuple-element.7.unit, f32[8,1024]{1,0:T(8,128)S(1)} %get-tuple-element.8.best, bf16[256,512]{1,0:T(8,128)(2,1)S(1)} %collective-permute-done.4.four), custom_call_target="tpu_custom_call" | custom-call | flops 1000000000 | bytes 4194304 | tf_op jit(solution)/shard_map/far/pallas_call | solution.py:130
  51.6 6.7 %all_to_all.15 = f32[4,2,128]{2,1,0:T(2,128)S(1)} all-to-all(f32[4,2,128]{2,1,0:T(2,128)S(1)} %far.1), channel_id=1, replica_groups=mesh['z'=8,'xl'=2,'c'=2,'y'=8,'xh'=2] {'xl','c'}, dimensions={0} | all-to-all | bytes 8192 | tf_op jit(solution)/shard_map/all_to_all | solution.py:172
  58.3 0.6 reduce_max.9
  (1 shorter events, 0.0 us)
Async XLA Ops:
  8.9 21.1 %collective-permute-start.1 = (bf16[512,512]{1,0:T(8,128)(2,1)S(1)}, bf16[512,512]{1,0:T(8,128)(2,1)S(1)}, u32[]{:S(2)}, u32[]{:S(2)}) collective-permute-start(bf16[512,512]{1,0:T(8,128)(2,1)S(1)} %bitcast.5), channel_id=1, source_target_pairs={{0,128},{16,400},{64,192},{80,464},{128,256},{144,16},{192,320},{2... | collective-permute-start | bytes 1572872 | tf_op jit(solution)/shard_map/ppermute | solution.py:160
  14.9 18.8 %all-to-all-start = ((f32[32,4,128]{2,1,0:T(4,128)}), f32[32,4,128]{2,1,0:T(4,128)S(1)}, u32[]{:S(2)}, u32[]{:S(2)}) async-start(f32[32,4,128]{2,1,0:T(4,128)} %broadcast_in_dim.8), calls=%async_computation | async-start | bytes 131072 | tf_op jit(solution)/shard_map/all_to_all | solution.py:25
  24.6 22.2 %collective-permute-start = (bf16[512,512]{1,0:T(8,128)(2,1)S(1)}, bf16[512,512]{1,0:T(8,128)(2,1)S(1)}, u32[]{:S(2)}, u32[]{:S(2)}) collective-permute-start(bf16[512,512]{1,0:T(8,128)(2,1)S(1)} %bitcast.6), channel_id=1, source_target_pairs={{0,32},{32,0},{1,33},{33,1},{2,34},{34,2},{3,35},{35,3},{4,36},{36... | collective-permute-start | bytes 1572872 | tf_op jit(solution)/shard_map/ppermute | solution.py:162
  27.8 19.1 %collective-permute-start.2 = (bf16[512,512]{1,0:T(8,128)(2,1)S(1)}, bf16[512,512]{1,0:T(8,128)(2,1)S(1)}, u32[]{:S(2)}, u32[]{:S(2)}) collective-permute-start(bf16[512,512]{1,0:T(8,128)(2,1)S(1)} %bitcast.7), channel_id=1, source_target_pairs={{0,64},{16,464},{64,128},{80,16},{128,192},{144,80},{192,256},{208... | collective-permute-start | bytes 1572872 | tf_op jit(solution)/shard_map/ppermute | solution.py:161
  30.0 16.9 %collective-permute-start.3 = (bf16[512,512]{1,0:T(8,128)(2,1)S(1)}, bf16[512,512]{1,0:T(8,128)(2,1)S(1)}, u32[]{:S(2)}, u32[]{:S(2)}) collective-permute-start(bf16[512,512]{1,0:T(8,128)(2,1)S(1)} %collective-permute-done.1.two), channel_id=1, source_target_pairs={{0,64},{16,464},{64,128},{80,16},{128,192},{144,80},{192,256},{208... | collective-permute-start | bytes 1572872 | tf_op jit(solution)/shard_map/ppermute | solution.py:165
  34.3 12.5 %all-to-all-start.1 = ((f32[8,4,128]{2,1,0:T(4,128)}), f32[8,4,128]{2,1,0:T(4,128)S(1)}, u32[]{:S(2)}, u32[]{:S(2)}) async-start(f32[8,4,128]{2,1,0:T(4,128)} %resend.1), calls=%async_computation.1 | async-start | bytes 32768 | tf_op jit(solution)/shard_map/all_to_all | solution.py:169
  37.7 9.2 %copy-start = (bf16[1,256,512]{2,1,0:T(8,128)(2,1)S(1)}, bf16[1,256,512]{2,1,0:T(8,128)(2,1)}, u32[]{:S(2)}) copy-start(bf16[1,256,512]{2,1,0:T(8,128)(2,1)} %param.3) | copy-start | bytes 786436
  37.7 9.1 %copy-start.1 = (s32[1,2,8]{2,1,0:T(2,128)S(1)}, s32[1,2,8]{2,1,0:T(2,128)}, u32[]{:S(2)}) copy-start(s32[1,2,8]{2,1,0:T(2,128)} %bounds.3) | copy-start | bytes 196
  37.7 12.8 %collective-permute-start.4 = (bf16[256,512]{1,0:T(8,128)(2,1)S(1)}, bf16[256,512]{1,0:T(8,128)(2,1)S(1)}, u32[]{:S(2)}, u32[]{:S(2)}) collective-permute-start(bf16[256,512]{1,0:T(8,128)(2,1)S(1)} %constant_dynamic-slice_fusion), channel_id=1, source_target_pairs={{0,128},{16,400},{64,192},{80,464},{128,256},{144,16},{192,320},{2... | collective-permute-start | bytes 786440 | tf_op jit(solution)/shard_map/ppermute | solution.py:168

commit v5 on v4

--- a/solution.py
+++ b/solution.py
@@ -158,14 +158,15 @@
     own = embeddings[0]
     chip = lax.all_gather(own, "c", axis=0, tiled=True)
     two = lax.ppermute(chip, ("z", "c"), shift((2, -2)))
-    one = lax.ppermute(chip, ("z", "c"), shift((1, -1)))
     side = lax.ppermute(chip, "xl", [(0, 1), (1, 0)])
     column_sums = jnp.sum(chip, axis=0, dtype=jnp.float32).reshape(4, 128)
     sums = spread_sum(column_sums, ("xl", "y", "xh"), XL * Y * XH)
+    later, two = lax.optimization_barrier((chip, two))
+    one = lax.ppermute(later, ("z", "c"), shift((1, -1)))
     three = lax.ppermute(two, ("z", "c"), shift((1, -1)))
     sums = resend(sums, Z, 8000000000)
-    half = lax.dynamic_slice_in_dim(two, lax.axis_index("c") * ROWS, ROWS, 0)
-    four = lax.ppermute(half, ("z", "c"), shift((2, -2)))
+    half = lax.dynamic_slice_in_dim(three, lax.axis_index("c") * ROWS, ROWS, 0)
+    four = lax.ppermute(half, ("z", "c"), shift((1, -1)))
     partials = lax.all_to_all(sums, "z", 0, 0)
     unit, best = near(cluster_rows, partials, own, chip, side, two, one, three)
     best = far(cluster_rows, partials, unit, best, four)

time: 59.3 us -> 59.4 us (level)
  waiting for transfers between devices: 5.12 us -> 2.19 us
  blocking collectives: 15.6 us -> 17.6 us
  starting transfers between devices: 31.3 us -> 32.3 us
    all_to_all x1, blocking collectives: 6.67 us -> 8.71 us  [on_device(): best = lax.all_to_all(best, ('xl', 'c'), 0, 0)]
    all_to_all x1, waiting for transfers between devices: 1.56 us -> 0.01 us  [spread_sum(): lax.all_to_all(jnp.broadcast_to(partial[None], (count, 4, 128)), axes, 0, 0)]
    all_to_all x1, waiting for transfers between devices: 3.55 us -> 2.17 us  [on_device(): partials = lax.all_to_all(sums, 'z', 0, 0)]
    ppermute x1, starting transfers between devices: 2.18 us -> 3.1 us  [on_device(): three = lax.ppermute(two, ('z', 'c'), shift((1, -1)))]
  transfers between devices with their start and end apart: 7 -> 7, of which waited for: 2 -> 1; matrix products, arithmetic and copies ran while one was open for 1% -> 1% of each run, Pallas kernels for 7% -> 7%
where the time goes in v5:
time: 59.4 us; the launch traced here: 59 us
  starting transfers between devices  32.3 us (54%)
  blocking collectives  17.6 us (30%)
  Pallas kernels  5.39 us (9%)
  waiting for transfers between devices  2.19 us (4%)
  other arithmetic  0.69 us (1%)
  local copies, waits for them, and re-layouts  0.68 us (1%)
    all_to_all x1, starting transfers between devices, spread_sum(): lax.all_to_all(jnp.broadcast_to(partial[None], (count, 4, 128)), axes, 0, 0)  9.67 us
    all_gather x1, blocking collectives, on_device(): chip = lax.all_gather(own, 'c', axis=0, tiled=True)  8.89 us
    all_to_all x1, blocking collectives, on_device(): best = lax.all_to_all(best, ('xl', 'c'), 0, 0)  8.71 us
    ppermute x1, starting transfers between devices, on_device(): two = lax.ppermute(chip, ('z', 'c'), shift((2, -2)))  5.27 us
    ppermute x1, starting transfers between devices, on_device(): four = lax.ppermute(half, ('z', 'c'), shift((1, -1)))  4.64 us
    pallas_call x1, Pallas kernels, near(): pl.pallas_call(near_kernel, out_shape=(jax.ShapeDtypeStruct((PLANE, D), j...  3.67 us
    all_to_all x1, starting transfers between devices, on_device(): partials = lax.all_to_all(sums, 'z', 0, 0)  3.33 us
    ppermute x1, starting transfers between devices, on_device(): side = lax.ppermute(chip, 'xl', [(0, 1), (1, 0)])  3.15 us
  transfers between devices with their start and end apart: 7, of which 1 were waited for; matrix products, arithmetic and copies ran while one was open for 1% of the time, Pallas kernels for 7%

profile of v5, /device:TPU:1, one launch (start us, length us, event | category | flops | bytes accessed | tf_op | source)
XLA Modules:
  0.0 59.0 jit_solution(7508141581689471705)
XLA Ops:
  0.0 8.9 %all-gather = bf16[1,512,512]{2,1,0:T(8,128)(2,1)S(1)} all-gather(bf16[1,256,512]{2,1,0:T(8,128)(2,1)} %param.3), channel_id=2, replica_groups=mesh['z'=8,'xl'=2,'c'=2,'y'=8,'xh'=2] {'c'}, dimensions={1}, use_global_device_ids=true | all-gather | bytes 786432 | tf_op jit(solution)/shard_map/all_gather | solution.py:159
  8.9 5.3 %collective-permute-start.1 = (bf16[512,512]{1,0:T(8,128)(2,1)S(1)}, bf16[512,512]{1,0:T(8,128)(2,1)S(1)}, u32[]{:S(2)}, u32[]{:S(2)}) collective-permute-start(bf16[512,512]{1,0:T(8,128)(2,1)S(1)} %bitcast.5), channel_id=1, source_target_pairs={{0,128},{16,400},{64,192},{80,464},{128,256},{144,16},{192,320},{2... | collective-permute-start | bytes 1572872 | tf_op jit(solution)/shard_map/ppermute | solution.py:160
  14.2 0.1 convert_reduce_fusion
  14.3 0.6 %broadcast_in_dim.8 = f32[32,4,128]{2,1,0:T(4,128)} broadcast(f32[4,128]{1,0:T(4,128)S(1)} %bitcast.10), dimensions={1,2} | broadcast | bytes 67584 | tf_op jit(solution)/shard_map/broadcast_in_dim | solution.py:25
  14.9 9.7 %all-to-all-start = ((f32[32,4,128]{2,1,0:T(4,128)}), f32[32,4,128]{2,1,0:T(4,128)S(1)}, u32[]{:S(2)}, u32[]{:S(2)}) async-start(f32[32,4,128]{2,1,0:T(4,128)} %broadcast_in_dim.8), calls=%async_computation | async-start | bytes 131072 | tf_op jit(solution)/shard_map/all_to_all | solution.py:25
  24.6 3.1 %collective-permute-start = (bf16[512,512]{1,0:T(8,128)(2,1)S(1)}, bf16[512,512]{1,0:T(8,128)(2,1)S(1)}, u32[]{:S(2)}, u32[]{:S(2)}) collective-permute-start(bf16[512,512]{1,0:T(8,128)(2,1)S(1)} %bitcast.6), channel_id=1, source_target_pairs={{0,32},{32,0},{1,33},{33,1},{2,34},{34,2},{3,35},{35,3},{4,36},{36... | collective-permute-start | bytes 1572872 | tf_op jit(solution)/shard_map/ppermute | solution.py:161
  27.8 0.0 collective-permute-done.1.two
  27.8 3.1 %collective-permute-start.3 = (bf16[512,512]{1,0:T(8,128)(2,1)S(1)}, bf16[512,512]{1,0:T(8,128)(2,1)S(1)}, u32[]{:S(2)}, u32[]{:S(2)}) collective-permute-start(bf16[512,512]{1,0:T(8,128)(2,1)S(1)} %collective-permute-done.1.two), channel_id=1, source_target_pairs={{0,64},{16,464},{64,128},{80,16},{128,192},{144,80},{192,256},{208... | collective-permute-start | bytes 1572872 | tf_op jit(solution)/shard_map/ppermute | solution.py:166
  30.9 3.1 %collective-permute-start.2 = (bf16[512,512]{1,0:T(8,128)(2,1)S(1)}, bf16[512,512]{1,0:T(8,128)(2,1)S(1)}, u32[]{:S(2)}, u32[]{:S(2)}) collective-permute-start(bf16[512,512]{1,0:T(8,128)(2,1)S(1)} %bitcast.7), channel_id=1, source_target_pairs={{0,64},{16,464},{64,128},{80,16},{128,192},{144,80},{192,256},{208... | collective-permute-start | bytes 1572872 | tf_op jit(solution)/shard_map/ppermute | solution.py:165
  34.0 0.0 all-to-all-done.received
  34.0 0.6 %resend.1 = f32[8,4,128]{2,1,0:T(4,128)} custom-call(f32[32,4,128]{2,1,0:T(4,128)S(1)} %all-to-all-done.received), custom_call_target="tpu_custom_call" | custom-call | flops 8000000000 | bytes 4194304 | tf_op jit(solution)/shard_map/resend/pallas_call | solution.py:146
  34.7 3.3 %all-to-all-start.1 = ((f32[8,4,128]{2,1,0:T(4,128)}), f32[8,4,128]{2,1,0:T(4,128)S(1)}, u32[]{:S(2)}, u32[]{:S(2)}) async-start(f32[8,4,128]{2,1,0:T(4,128)} %resend.1), calls=%async_computation.1 | async-start | bytes 32768 | tf_op jit(solution)/shard_map/all_to_all | solution.py:170
  38.0 0.0 copy-start
  38.0 0.0 collective-permute-done.3.three
  38.1 0.0 copy-start.1
  38.1 4.6 %collective-permute-start.4 = (bf16[256,512]{1,0:T(8,128)(2,1)S(1)}, bf16[256,512]{1,0:T(8,128)(2,1)S(1)}, u32[]{:S(2)}, u32[]{:S(2)}) collective-permute-start(bf16[256,512]{1,0:T(8,128)(2,1)S(1)} %constant_dynamic-slice_fusion), channel_id=1, source_target_pairs={{0,64},{16,464},{64,128},{80,16},{128,192},{144,80},{192,256},{208... | collective-permute-start | bytes 786440 | tf_op jit(solution)/shard_map/ppermute | solution.py:169
  42.7 2.2 %all-to-all-done.1.partials = f32[8,4,128]{2,1,0:T(4,128)S(1)} async-done(((f32[8,4,128]{2,1,0:T(4,128)}), f32[8,4,128]{2,1,0:T(4,128)S(1)}, u32[]{:S(2)}, u32[]{:S(2)}) %all-to-all-start.1) | async-done | bytes 16416 | tf_op jit(solution)/shard_map/all_to_all | solution.py:170
  44.9 0.0 collective-permute-done.side
  44.9 0.0 collective-permute-done.2.one
  44.9 0.0 copy-done
  44.9 0.0 copy-done.1
  44.9 3.7 %near.1 = (bf16[1024,512]{1,0:T(8,128)(2,1)S(1)}, f32[8,1024]{1,0:T(8,128)S(1)}) custom-call(s32[1,2,8]{2,1,0:T(2,128)S(1)} %copy-done.1, f32[8,4,128]{2,1,0:T(4,128)S(1)} %all-to-all-done.1.partials, bf16[256,512]{1,0:T(8,128)(2,1)S(1)} %bitcast.9, bf16[512,512]{1,0:T(8,128)(2,1)S(1)} %bitcast.8, bf16[512,512]{1,0:T(8,128)(2,1)S(1)} %collective-permute-done.side, ...), custom_call_target="tpu_custom_call" | custom-call | flops 5000000000 | bytes 4194304 | tf_op jit(solution)/shard_map/near/pallas_call | solution.py:114
  48.6 0.0 collective-permute-done.4.four
  48.6 1.1 %far.1 = f32[4,2,128]{2,1,0:T(2,128)S(1)} custom-call(s32[1,2,8]{2,1,0:T(2,128)S(1)} %copy-done.1, f32[8,4,128]{2,1,0:T(4,128)S(1)} %all-to-all-done.1.partials, bf16[1024,512]{1,0:T(8,128)(2,1)S(1)} %get-tuple-element.11.unit, f32[8,1024]{1,0:T(8,128)S(1)} %get-tuple-element.12.best, bf16[256,512]{1,0:T(8,128)(2,1)S(1)} %collective-permute-done.4.four), custom_call_target="tpu_custom_call" | custom-call | flops 1000000000 | bytes 4194304 | tf_op jit(solution)/shard_map/far/pallas_call | solution.py:130
  49.7 8.7 %all_to_all.15 = f32[4,2,128]{2,1,0:T(2,128)S(1)} all-to-all(f32[4,2,128]{2,1,0:T(2,128)S(1)} %far.1), channel_id=1, replica_groups=mesh['z'=8,'xl'=2,'c'=2,'y'=8,'xh'=2] {'xl','c'}, dimensions={0} | all-to-all | bytes 8192 | tf_op jit(solution)/shard_map/all_to_all | solution.py:173
  58.4 0.6 reduce_max.9
  (1 shorter events, 0.0 us)
Async XLA Ops:
  8.9 18.9 %collective-permute-start.1 = (bf16[512,512]{1,0:T(8,128)(2,1)S(1)}, bf16[512,512]{1,0:T(8,128)(2,1)S(1)}, u32[]{:S(2)}, u32[]{:S(2)}) collective-permute-start(bf16[512,512]{1,0:T(8,128)(2,1)S(1)} %bitcast.5), channel_id=1, source_target_pairs={{0,128},{16,400},{64,192},{80,464},{128,256},{144,16},{192,320},{2... | collective-permute-start | bytes 1572872 | tf_op jit(solution)/shard_map/ppermute | solution.py:160
  14.9 19.1 %all-to-all-start = ((f32[32,4,128]{2,1,0:T(4,128)}), f32[32,4,128]{2,1,0:T(4,128)S(1)}, u32[]{:S(2)}, u32[]{:S(2)}) async-start(f32[32,4,128]{2,1,0:T(4,128)} %broadcast_in_dim.8), calls=%async_computation | async-start | bytes 131072 | tf_op jit(solution)/shard_map/all_to_all | solution.py:25
  24.6 20.3 %collective-permute-start = (bf16[512,512]{1,0:T(8,128)(2,1)S(1)}, bf16[512,512]{1,0:T(8,128)(2,1)S(1)}, u32[]{:S(2)}, u32[]{:S(2)}) collective-permute-start(bf16[512,512]{1,0:T(8,128)(2,1)S(1)} %bitcast.6), channel_id=1, source_target_pairs={{0,32},{32,0},{1,33},{33,1},{2,34},{34,2},{3,35},{35,3},{4,36},{36... | collective-permute-start | bytes 1572872 | tf_op jit(solution)/shard_map/ppermute | solution.py:161
  27.8 10.2 %collective-permute-start.3 = (bf16[512,512]{1,0:T(8,128)(2,1)S(1)}, bf16[512,512]{1,0:T(8,128)(2,1)S(1)}, u32[]{:S(2)}, u32[]{:S(2)}) collective-permute-start(bf16[512,512]{1,0:T(8,128)(2,1)S(1)} %collective-permute-done.1.two), channel_id=1, source_target_pairs={{0,64},{16,464},{64,128},{80,16},{128,192},{144,80},{192,256},{208... | collective-permute-start | bytes 1572872 | tf_op jit(solution)/shard_map/ppermute | solution.py:166
  30.9 14.0 %collective-permute-start.2 = (bf16[512,512]{1,0:T(8,128)(2,1)S(1)}, bf16[512,512]{1,0:T(8,128)(2,1)S(1)}, u32[]{:S(2)}, u32[]{:S(2)}) collective-permute-start(bf16[512,512]{1,0:T(8,128)(2,1)S(1)} %bitcast.7), channel_id=1, source_target_pairs={{0,64},{16,464},{64,128},{80,16},{128,192},{144,80},{192,256},{208... | collective-permute-start | bytes 1572872 | tf_op jit(solution)/shard_map/ppermute | solution.py:165
  34.7 10.2 %all-to-all-start.1 = ((f32[8,4,128]{2,1,0:T(4,128)}), f32[8,4,128]{2,1,0:T(4,128)S(1)}, u32[]{:S(2)}, u32[]{:S(2)}) async-start(f32[8,4,128]{2,1,0:T(4,128)} %resend.1), calls=%async_computation.1 | async-start | bytes 32768 | tf_op jit(solution)/shard_map/all_to_all | solution.py:170
  38.0 6.9 %copy-start = (bf16[1,256,512]{2,1,0:T(8,128)(2,1)S(1)}, bf16[1,256,512]{2,1,0:T(8,128)(2,1)}, u32[]{:S(2)}) copy-start(bf16[1,256,512]{2,1,0:T(8,128)(2,1)} %param.3) | copy-start | bytes 786436
  38.1 6.8 %copy-start.1 = (s32[1,2,8]{2,1,0:T(2,128)S(1)}, s32[1,2,8]{2,1,0:T(2,128)}, u32[]{:S(2)}) copy-start(s32[1,2,8]{2,1,0:T(2,128)} %bounds.3) | copy-start | bytes 196
  38.1 10.5 %collective-permute-start.4 = (bf16[256,512]{1,0:T(8,128)(2,1)S(1)}, bf16[256,512]{1,0:T(8,128)(2,1)S(1)}, u32[]{:S(2)}, u32[]{:S(2)}) collective-permute-start(bf16[256,512]{1,0:T(8,128)(2,1)S(1)} %constant_dynamic-slice_fusion), channel_id=1, source_target_pairs={{0,64},{16,464},{64,128},{80,16},{128,192},{144,80},{192,256},{208... | collective-permute-start | bytes 786440 | tf_op jit(solution)/shard_map/ppermute | solution.py:169

commit v6 on v5

--- a/solution.py
+++ b/solution.py
@@ -21,10 +21,6 @@
     return [(z * C + c, (z + hops[c]) % Z * C + c) for z in range(Z) for c in range(C)]
 
 
-def spread_sum(partial, axes, count):
-    return lax.all_to_all(jnp.broadcast_to(partial[None], (count, 4, 128)), axes, 0, 0)
-
-
 def plane_start(z, xl, offset):
     return lax.rem(z + offset + Z, Z) * PLANE + xl * CHIP
 
@@ -53,12 +49,12 @@
     return z * PLANE + jnp.where(lane < CHIP, xl * CHIP + lane, lane - xl * CHIP)
 
 
-def near_kernel(bounds, partials, own, chip, side, two, one, three, unit, best, cols):
+def near_kernel(bounds, partials, chip, side, two, one, three, unit, best, cols):
     z, xl, core = lax.axis_index("z"), lax.axis_index("xl"), lax.axis_index("c")
     sign = 2 * core - 1
     normalized = normalizer(partials)
     starts = [plane_start(z, xl, 0) + core * ROWS]
-    cols[pl.ds(0, ROWS)] = normalized(own[...])
+    cols[pl.ds(0, ROWS)] = normalized(chip[pl.ds(pl.multiple_of(core * ROWS, ROWS), ROWS)])
     for block, hops in ((two, 2), (one, 1), (three, 3)):
         for k in range(CHIP // STEP):
             cols[pl.ds(len(starts) * STEP, STEP)] = normalized(block[pl.ds(k * STEP, STEP)])
@@ -154,13 +150,28 @@
     )(received)
 
 
+def first_sums(chip, count):
+    def kernel(chip, out):
+        total = jnp.sum(chip[...].astype(jnp.float32), axis=0, keepdims=True)
+        parts = jnp.concatenate([total[:, k * 128 : (k + 1) * 128] for k in range(4)], axis=0)
+        out[...] = jnp.broadcast_to(parts[None], out.shape)
+
+    return pl.pallas_call(
+        kernel,
+        out_shape=jax.ShapeDtypeStruct((count, 4, 128), jnp.float32),
+        in_specs=[IN_VMEM],
+        out_specs=IN_VMEM,
+        compiler_params=pltpu.CompilerParams(vmem_limit_bytes=4 * 1024 * 1024),
+        cost_estimate=cost(1e8),
+        name="first_sums",
+    )(chip)
+
+
 def on_device(embeddings, cluster_rows):
-    own = embeddings[0]
-    chip = lax.all_gather(own, "c", axis=0, tiled=True)
+    chip = lax.all_gather(embeddings[0], "c", axis=0, tiled=True)
     two = lax.ppermute(chip, ("z", "c"), shift((2, -2)))
     side = lax.ppermute(chip, "xl", [(0, 1), (1, 0)])
-    column_sums = jnp.sum(chip, axis=0, dtype=jnp.float32).reshape(4, 128)
-    sums = spread_sum(column_sums, ("xl", "y", "xh"), XL * Y * XH)
+    sums = lax.all_to_all(first_sums(chip, XL * Y * XH), ("xl", "y", "xh"), 0, 0)
     later, two = lax.optimization_barrier((chip, two))
     one = lax.ppermute(later, ("z", "c"), shift((1, -1)))
     three = lax.ppermute(two, ("z", "c"), shift((1, -1)))
@@ -168,7 +179,7 @@
     half = lax.dynamic_slice_in_dim(three, lax.axis_index("c") * ROWS, ROWS, 0)
     four = lax.ppermute(half, ("z", "c"), shift((1, -1)))
     partials = lax.all_to_all(sums, "z", 0, 0)
-    unit, best = near(cluster_rows, partials, own, chip, side, two, one, three)
+    unit, best = near(cluster_rows, partials, chip, side, two, one, three)
     best = far(cluster_rows, partials, unit, best, four)
     best = lax.all_to_all(best, ("xl", "c"), 0, 0)
     return jnp.max(best, axis=0).reshape(1, ROWS)

time: 59.4 us -> 59.4 us (level)
  Pallas kernels: 5.39 us -> 6.11 us
  local copies, waits for them, and re-layouts: 0.68 us -> 0.03 us
    pallas_call x0 -> x1, Pallas kernels: none -> 0.72 us  [first_sums(): pl.pallas_call(kernel, out_shape=jax.ShapeDtypeStruct((count, 4, 128), jn...]
    broadcast_in_dim x1 -> x0, local copies, waits for them, and re-layouts: 0.64 us -> none  [spread_sum(): jnp.broadcast_to(partial[None], (count, 4, 128))]
  transfers between devices with their start and end apart: 7 -> 7, of which waited for: 1 -> 1; matrix products, arithmetic and copies ran while one was open for 1% -> 0% of each run, Pallas kernels for 7% -> 9%
where the time goes in v6:
time: 59.4 us; the launch traced here: 59 us
  starting transfers between devices  32.2 us (54%)
  blocking collectives  17.6 us (30%)
  Pallas kernels  6.11 us (10%)
  waiting for transfers between devices  2.33 us (4%)
    all_to_all x1, starting transfers between devices, on_device(): lax.all_to_all(first_sums(chip, XL * Y * XH), ('xl', 'y', 'xh'), 0, 0)  9.67 us
    all_gather x1, blocking collectives, on_device(): chip = lax.all_gather(embeddings[0], 'c', axis=0, tiled=True)  8.89 us
    all_to_all x1, blocking collectives, on_device(): best = lax.all_to_all(best, ('xl', 'c'), 0, 0)  8.71 us
    ppermute x1, starting transfers between devices, on_device(): two = lax.ppermute(chip, ('z', 'c'), shift((2, -2)))  5.27 us
    ppermute x1, starting transfers between devices, on_device(): four = lax.ppermute(half, ('z', 'c'), shift((1, -1)))  4.51 us
    pallas_call x1, Pallas kernels, near(): pl.pallas_call(near_kernel, out_shape=(jax.ShapeDtypeStruct((PLANE, D), j...  3.68 us
    all_to_all x1, starting transfers between devices, on_device(): partials = lax.all_to_all(sums, 'z', 0, 0)  3.34 us
    ppermute x1, starting transfers between devices, on_device(): side = lax.ppermute(chip, 'xl', [(0, 1), (1, 0)])  3.15 us
  transfers between devices with their start and end apart: 7, of which 1 were waited for; matrix products, arithmetic and copies ran while one was open for 0% of the time, Pallas kernels for 9%

profile of v6, /device:TPU:1, one launch (start us, length us, event | category | flops | bytes accessed | tf_op | source)
XLA Modules:
  0.0 59.0 jit_solution(5514200651607533894)
XLA Ops:
  0.0 8.9 %all-gather = bf16[1,512,512]{2,1,0:T(8,128)(2,1)S(1)} all-gather(bf16[1,256,512]{2,1,0:T(8,128)(2,1)} %param.3), channel_id=2, replica_groups=mesh['z'=8,'xl'=2,'c'=2,'y'=8,'xh'=2] {'c'}, dimensions={1}, use_global_device_ids=true | all-gather | bytes 786432 | tf_op jit(solution)/shard_map/all_gather | solution.py:171
  8.9 5.3 %collective-permute-start.1 = (bf16[512,512]{1,0:T(8,128)(2,1)S(1)}, bf16[512,512]{1,0:T(8,128)(2,1)S(1)}, u32[]{:S(2)}, u32[]{:S(2)}) collective-permute-start(bf16[512,512]{1,0:T(8,128)(2,1)S(1)} %bitcast.2), channel_id=1, source_target_pairs={{0,128},{16,400},{64,192},{80,464},{128,256},{144,16},{192,320},{2... | collective-permute-start | bytes 1572872 | tf_op jit(solution)/shard_map/ppermute | solution.py:172
  14.2 0.7 %first_sums.1 = f32[32,4,128]{2,1,0:T(4,128)} custom-call(bf16[512,512]{1,0:T(8,128)(2,1)S(1)} %bitcast.3), custom_call_target="tpu_custom_call" | custom-call | flops 100000000 | bytes 4194304 | tf_op jit(solution)/shard_map/first_sums/pallas_call | solution.py:159
  14.9 9.7 %all-to-all-start = ((f32[32,4,128]{2,1,0:T(4,128)}), f32[32,4,128]{2,1,0:T(4,128)S(1)}, u32[]{:S(2)}, u32[]{:S(2)}) async-start(f32[32,4,128]{2,1,0:T(4,128)} %first_sums.1), calls=%async_computation | async-start | bytes 131072 | tf_op jit(solution)/shard_map/all_to_all | solution.py:174
  24.6 3.1 %collective-permute-start = (bf16[512,512]{1,0:T(8,128)(2,1)S(1)}, bf16[512,512]{1,0:T(8,128)(2,1)S(1)}, u32[]{:S(2)}, u32[]{:S(2)}) collective-permute-start(bf16[512,512]{1,0:T(8,128)(2,1)S(1)} %bitcast.4), channel_id=1, source_target_pairs={{0,32},{32,0},{1,33},{33,1},{2,34},{34,2},{3,35},{35,3},{4,36},{36... | collective-permute-start | bytes 1572872 | tf_op jit(solution)/shard_map/ppermute | solution.py:173
  27.7 0.0 collective-permute-done.1.two
  27.7 3.1 %collective-permute-start.3 = (bf16[512,512]{1,0:T(8,128)(2,1)S(1)}, bf16[512,512]{1,0:T(8,128)(2,1)S(1)}, u32[]{:S(2)}, u32[]{:S(2)}) collective-permute-start(bf16[512,512]{1,0:T(8,128)(2,1)S(1)} %collective-permute-done.1.two), channel_id=1, source_target_pairs={{0,64},{16,464},{64,128},{80,16},{128,192},{144,80},{192,256},{208... | collective-permute-start | bytes 1572872 | tf_op jit(solution)/shard_map/ppermute | solution.py:177
  30.9 3.1 %collective-permute-start.2 = (bf16[512,512]{1,0:T(8,128)(2,1)S(1)}, bf16[512,512]{1,0:T(8,128)(2,1)S(1)}, u32[]{:S(2)}, u32[]{:S(2)}) collective-permute-start(bf16[512,512]{1,0:T(8,128)(2,1)S(1)} %bitcast.5), channel_id=1, source_target_pairs={{0,64},{16,464},{64,128},{80,16},{128,192},{144,80},{192,256},{208... | collective-permute-start | bytes 1572872 | tf_op jit(solution)/shard_map/ppermute | solution.py:176
  34.0 0.0 all-to-all-done.received
  34.0 0.6 %resend.1 = f32[8,4,128]{2,1,0:T(4,128)} custom-call(f32[32,4,128]{2,1,0:T(4,128)S(1)} %all-to-all-done.received), custom_call_target="tpu_custom_call" | custom-call | flops 8000000000 | bytes 4194304 | tf_op jit(solution)/shard_map/resend/pallas_call | solution.py:142
  34.6 3.3 %all-to-all-start.1 = ((f32[8,4,128]{2,1,0:T(4,128)}), f32[8,4,128]{2,1,0:T(4,128)S(1)}, u32[]{:S(2)}, u32[]{:S(2)}) async-start(f32[8,4,128]{2,1,0:T(4,128)} %resend.1), calls=%async_computation.1 | async-start | bytes 32768 | tf_op jit(solution)/shard_map/all_to_all | solution.py:181
  38.0 0.0 copy-start
  38.0 0.0 collective-permute-done.3.three
  38.1 4.5 %collective-permute-start.4 = (bf16[256,512]{1,0:T(8,128)(2,1)S(1)}, bf16[256,512]{1,0:T(8,128)(2,1)S(1)}, u32[]{:S(2)}, u32[]{:S(2)}) collective-permute-start(bf16[256,512]{1,0:T(8,128)(2,1)S(1)} %constant_dynamic-slice_fusion), channel_id=1, source_target_pairs={{0,64},{16,464},{64,128},{80,16},{128,192},{144,80},{192,256},{208... | collective-permute-start | bytes 786440 | tf_op jit(solution)/shard_map/ppermute | solution.py:180
  42.6 2.3 %all-to-all-done.1.partials = f32[8,4,128]{2,1,0:T(4,128)S(1)} async-done(((f32[8,4,128]{2,1,0:T(4,128)}), f32[8,4,128]{2,1,0:T(4,128)S(1)}, u32[]{:S(2)}, u32[]{:S(2)}) %all-to-all-start.1) | async-done | bytes 16416 | tf_op jit(solution)/shard_map/all_to_all | solution.py:181
  44.9 0.0 collective-permute-done.side
  44.9 0.0 collective-permute-done.2.one
  44.9 0.0 copy-done
  44.9 3.7 %near.1 = (bf16[1024,512]{1,0:T(8,128)(2,1)S(1)}, f32[8,1024]{1,0:T(8,128)S(1)}) custom-call(s32[1,2,8]{2,1,0:T(2,128)S(1)} %copy-done, f32[8,4,128]{2,1,0:T(4,128)S(1)} %all-to-all-done.1.partials, bf16[512,512]{1,0:T(8,128)(2,1)S(1)} %bitcast.6, bf16[512,512]{1,0:T(8,128)(2,1)S(1)} %collective-permute-done.side, ...), custom_call_target="tpu_custom_call" | custom-call | flops 5000000000 | bytes 4194304 | tf_op jit(solution)/shard_map/near/pallas_call | solution.py:110
  48.6 0.0 collective-permute-done.4.four
  48.6 1.1 %far.1 = f32[4,2,128]{2,1,0:T(2,128)S(1)} custom-call(s32[1,2,8]{2,1,0:T(2,128)S(1)} %copy-done, f32[8,4,128]{2,1,0:T(4,128)S(1)} %all-to-all-done.1.partials, bf16[1024,512]{1,0:T(8,128)(2,1)S(1)} %get-tuple-element.11.unit, f32[8,1024]{1,0:T(8,128)S(1)} %get-tuple-element.12.best, bf16[256,512]{1,0:T(8,128)(2,1)S(1)} %collective-permute-done.4.four), custom_call_target="tpu_custom_call" | custom-call | flops 1000000000 | bytes 4194304 | tf_op jit(solution)/shard_map/far/pallas_call | solution.py:126
  49.7 8.7 %all_to_all.15 = f32[4,2,128]{2,1,0:T(2,128)S(1)} all-to-all(f32[4,2,128]{2,1,0:T(2,128)S(1)} %far.1), channel_id=1, replica_groups=mesh['z'=8,'xl'=2,'c'=2,'y'=8,'xh'=2] {'xl','c'}, dimensions={0} | all-to-all | bytes 8192 | tf_op jit(solution)/shard_map/all_to_all | solution.py:184
  58.4 0.6 reduce_max.9
  (1 shorter events, 0.0 us)
Async XLA Ops:
  8.9 18.8 %collective-permute-start.1 = (bf16[512,512]{1,0:T(8,128)(2,1)S(1)}, bf16[512,512]{1,0:T(8,128)(2,1)S(1)}, u32[]{:S(2)}, u32[]{:S(2)}) collective-permute-start(bf16[512,512]{1,0:T(8,128)(2,1)S(1)} %bitcast.2), channel_id=1, source_target_pairs={{0,128},{16,400},{64,192},{80,464},{128,256},{144,16},{192,320},{2... | collective-permute-start | bytes 1572872 | tf_op jit(solution)/shard_map/ppermute | solution.py:172
  14.9 19.1 %all-to-all-start = ((f32[32,4,128]{2,1,0:T(4,128)}), f32[32,4,128]{2,1,0:T(4,128)S(1)}, u32[]{:S(2)}, u32[]{:S(2)}) async-start(f32[32,4,128]{2,1,0:T(4,128)} %first_sums.1), calls=%async_computation | async-start | bytes 131072 | tf_op jit(solution)/shard_map/all_to_all | solution.py:174
  24.6 20.3 %collective-permute-start = (bf16[512,512]{1,0:T(8,128)(2,1)S(1)}, bf16[512,512]{1,0:T(8,128)(2,1)S(1)}, u32[]{:S(2)}, u32[]{:S(2)}) collective-permute-start(bf16[512,512]{1,0:T(8,128)(2,1)S(1)} %bitcast.4), channel_id=1, source_target_pairs={{0,32},{32,0},{1,33},{33,1},{2,34},{34,2},{3,35},{35,3},{4,36},{36... | collective-permute-start | bytes 1572872 | tf_op jit(solution)/shard_map/ppermute | solution.py:173
  27.7 10.3 %collective-permute-start.3 = (bf16[512,512]{1,0:T(8,128)(2,1)S(1)}, bf16[512,512]{1,0:T(8,128)(2,1)S(1)}, u32[]{:S(2)}, u32[]{:S(2)}) collective-permute-start(bf16[512,512]{1,0:T(8,128)(2,1)S(1)} %collective-permute-done.1.two), channel_id=1, source_target_pairs={{0,64},{16,464},{64,128},{80,16},{128,192},{144,80},{192,256},{208... | collective-permute-start | bytes 1572872 | tf_op jit(solution)/shard_map/ppermute | solution.py:177
  30.9 14.0 %collective-permute-start.2 = (bf16[512,512]{1,0:T(8,128)(2,1)S(1)}, bf16[512,512]{1,0:T(8,128)(2,1)S(1)}, u32[]{:S(2)}, u32[]{:S(2)}) collective-permute-start(bf16[512,512]{1,0:T(8,128)(2,1)S(1)} %bitcast.5), channel_id=1, source_target_pairs={{0,64},{16,464},{64,128},{80,16},{128,192},{144,80},{192,256},{208... | collective-permute-start | bytes 1572872 | tf_op jit(solution)/shard_map/ppermute | solution.py:176
  34.6 10.2 %all-to-all-start.1 = ((f32[8,4,128]{2,1,0:T(4,128)}), f32[8,4,128]{2,1,0:T(4,128)S(1)}, u32[]{:S(2)}, u32[]{:S(2)}) async-start(f32[8,4,128]{2,1,0:T(4,128)} %resend.1), calls=%async_computation.1 | async-start | bytes 32768 | tf_op jit(solution)/shard_map/all_to_all | solution.py:181
  38.0 6.9 %copy-start = (s32[1,2,8]{2,1,0:T(2,128)S(1)}, s32[1,2,8]{2,1,0:T(2,128)}, u32[]{:S(2)}) copy-start(s32[1,2,8]{2,1,0:T(2,128)} %bounds.3) | copy-start | bytes 196
  38.1 10.5 %collective-permute-start.4 = (bf16[256,512]{1,0:T(8,128)(2,1)S(1)}, bf16[256,512]{1,0:T(8,128)(2,1)S(1)}, u32[]{:S(2)}, u32[]{:S(2)}) collective-permute-start(bf16[256,512]{1,0:T(8,128)(2,1)S(1)} %constant_dynamic-slice_fusion), channel_id=1, source_target_pairs={{0,64},{16,464},{64,128},{80,16},{128,192},{144,80},{192,256},{208... | collective-permute-start | bytes 786440 | tf_op jit(solution)/shard_map/ppermute | solution.py:180
